TPU v7x, 32 devices: a whole 2x2x4 slice. The times are simulated.
32 devices in a mesh: pairs: 8 (over z, x), win: 4 (over y, core).
Axes of the slice: x: 2, y: 2, z: 4, core: 2. Of those that a mesh axis runs over, the one named last changes fastest.
Arguments:
- raw_traces: bfloat16 [4, 40, 128, 512], P('win', None, 'pairs'), may hold values from -6 to 6
- tile_pairs: int32 [8, 4, 2], replicated, may hold values from -1 to 39, as said below
- block_slot: int32 [40], replicated, may hold values from 0 to 39, as said below
- win_offset: int32 [4], P('win'), may hold values from 0 to 128
Outputs:
- stacks: float32 [128, 32, 128, 128], P('win', 'pairs')
Inputs may be any that keep to these rules, and one draw needn't show every extreme that they name: `tile_pairs`: row p lists owner p's tiles: pairs of block numbers, then rows of -1. Each owner has 1 to 4 tiles and some owner exactly 4. The blocks named in one owner's row are all different. `block_slot`: each slot holds exactly one block.
All inputs are finite; a program needn't handle non-finite values.
Results may differ from a plain program's by a relative error of at most 0.0041.
Values may be sent and summed in bfloat16 or wider, within the bound.
No kernel may reach another device: no remote copies, remote signals or barrier semaphores. Data moves between devices by JAX's collectives and lax.ppermute only.
A program may use at most 192 MiB of HBM per device.

v0:
```python
import math

import jax
import jax.numpy as jnp
from jax import lax
from jax.sharding import PartitionSpec as P

LAGS = 128


eps = 1e-06


def whiten(signal):
    length = signal.shape[-1]
    width = LAGS
    radius = LAGS // 2
    seg_count = length // width
    magnitude = jnp.abs(signal).reshape(signal.shape[:-1] + (seg_count, width))
    padded = jnp.pad(magnitude, [(0, 0)] * (magnitude.ndim - 2) + [(1, 1), (0, 0)])
    windows = jnp.concatenate([padded[..., :-2, :], padded[..., 1:-1, :], padded[..., 2:, :]], -1)
    rowpos = jnp.arange(3 * width)[:, None]
    colpos = jnp.arange(width)[None, :]
    band_matrix = (jnp.abs(rowpos - width - colpos) <= radius).astype(jnp.float32)
    totals = jnp.einsum(
        "...ni,ij->...nj", windows, band_matrix, precision=lax.Precision.HIGHEST
    ).reshape(signal.shape)
    position = jnp.arange(length)
    tally = (jnp.minimum(position, radius) + jnp.minimum(length - 1 - position, radius) + 1).astype(
        jnp.float32
    )
    return (signal / (totals / tally + eps)).astype(jnp.bfloat16)


def correlate(leading_blocks, trailing_blocks):
    seg_len = leading_blocks.shape[-1]
    samples = seg_len - LAGS
    half = LAGS // 2
    kernel = jnp.transpose(leading_blocks[..., half : half + samples], (1, 0, 2))
    source = jnp.transpose(trailing_blocks[..., : seg_len - 1], (1, 0, 2))
    return lax.conv_general_dilated(
        source,
        kernel,
        (1,),
        "VALID",
        dimension_numbers=("NCH", "OIH", "CNH"),
        preferred_element_type=jnp.float32,
    )


def body(raw_traces, tile_pairs, block_slot, win_offset):
    owner_index = lax.axis_index("pairs")
    pair_count = lax.axis_size("pairs")
    win_count = lax.axis_size("win")
    local_channels = raw_traces.shape[2]
    channels = local_channels * pair_count
    seg_len = raw_traces.shape[3] - LAGS
    samples = seg_len - LAGS
    tile_count = tile_pairs.shape[1]
    segment = lax.dynamic_slice_in_dim(raw_traces[0], win_offset[0], seg_len, 2).astype(jnp.float32)
    whitened = whiten(segment)
    wanted = tile_pairs.reshape(pair_count, 2 * tile_count)
    slot_index = block_slot[jnp.maximum(wanted, 0)]
    outgoing = jnp.take(whitened, slot_index.reshape(-1), axis=0).reshape(
        pair_count, 2 * tile_count, local_channels, seg_len
    )
    incoming = lax.all_to_all(outgoing, "pairs", split_axis=0, concat_axis=2, tiled=True)
    blocks = incoming[0].reshape(tile_count, 2, channels, seg_len)
    own_tiles = lax.dynamic_index_in_dim(tile_pairs, owner_index, 0, keepdims=False)
    tile_valid = (own_tiles[:, 0] >= 0).astype(jnp.float32)
    firsts = blocks[:, 0]
    seconds = blocks[:, 1]
    row_share = channels // win_count
    spread_rows = lax.all_to_all(firsts[:, None], "win", split_axis=2, concat_axis=1, tiled=True)
    initial = jnp.zeros((row_share, tile_count, channels, LAGS), jnp.float32)
    piece = lax.all_gather(seconds[:, None], "win", axis=1, tiled=True)
    summed = initial + jnp.stack(
        [correlate(spread_rows[tile], piece[tile]) for tile in range(tile_count)], 1
    )
    scale = 1.0 / math.sqrt(win_count * samples)
    return summed * scale * tile_valid[None, :, None, None]


def solution(mesh):
    return jax.shard_map(
        body,
        mesh=mesh,
        in_specs=(P("win", None, "pairs", None), P(), P(), P("win")),
        out_specs=P("win", "pairs", None, None),
        check_vma=False,
    )
```

profile of v0, /device:TPU:0, one launch (start us, length us, event | category | flops | bytes accessed | tf_op | source)
XLA Modules:
  0.0 110.5 jit_solution(11894649571355318988)
XLA Ops:
  6.6 0.8 broadcast_maximum_fusion
  7.4 0.1 reshape.108
  7.6 0.8 gather_fusion
  9.1 0.2 convert_abs_fusion
  9.4 0.4 abs.11
  9.9 0.1 pad_slice_fusion.1
  10.0 1.5 %fusion.6 = f32[40,3,2,8,128]{4,3,2,1,0:T(8,128)S(1)} fusion(f32[40,16,3,128]{3,1,2,0:T(8,128)S(1)} %get-tuple-element.10, f32[40,16,3,128]{3,1,2,0:T(8,128)S(1)} %copy.43, f32[40,16,3,128]{3,1,2,0:T(8,128)S(1)} %get-tuple-element.9, s32[384]{0:T(512)S(1)} %iota_add_fusion), kind=kOutput, calls=%fused_computation.15 | convolution fusion | flops 1134084096 | bytes 3933696 | tf_op jit(solution)/shard_map/...ni,ij->...nj/dot_general | solution.py:25
  11.6 0.4 fusion.10
  11.9 0.7 gather_fusion.1
  12.7 0.2 broadcast_select_fusion
  12.8 27.2 %all_to_all.24 = bf16[8,8,16,384]{3,2,1,0:T(8,128)(2,1)S(1)} all-to-all(bf16[8,8,16,384]{3,2,1,0:T(8,128)(2,1)S(1)} %broadcast_select_fusion), channel_id=1, replica_groups=mesh['pairs'=8,'win'=4] {'pairs'}, dimensions={0} | all-to-all | bytes 1572864 | tf_op jit(solution)/shard_map/all_to_all | solution.py:67
  40.1 0.8 slice_bitcast_fusion
  41.0 1.1 copy.49
  42.0 3.6 %all-to-all-start.1 = ((bf16[4,1,128,384]{3,0,1,2:T(4,128)(2,1)}), bf16[4,1,128,384]{3,0,1,2:T(4,128)(2,1)S(1)}, u32[]{:S(2)}, u32[]{:S(2)}) async-start(bf16[4,1,128,384]{3,0,1,2:T(4,128)(2,1)} %copy.49), calls=%async_computation.1 | async-start | bytes 786432 | tf_op jit(solution)/shard_map/all_to_all | solution.py:74
  45.9 10.6 %all-to-all-done.1 = bf16[4,1,128,384]{3,0,1,2:T(4,128)(2,1)S(1)} async-done(((bf16[4,1,128,384]{3,0,1,2:T(4,128)(2,1)}), bf16[4,1,128,384]{3,0,1,2:T(4,128)(2,1)S(1)}, u32[]{:S(2)}, u32[]{:S(2)}) %all-to-all-start.1) | async-done | bytes 393248 | tf_op jit(solution)/shard_map/all_to_all | solution.py:74
  56.5 0.6 fusion.29
  57.5 0.2 copy.75
  57.7 0.2 copy.69
  57.9 0.2 copy.72
  58.1 0.2 copy.66
  58.3 4.6 %all-gather.2.cloned.1.call-done = bf16[4,4,128,384]{3,2,0,1:T(8,128)(2,1)} async-done(((bf16[4,1,128,384]{3,2,0,1:T(8,128)(2,1)}), bf16[4,4,128,384]{3,2,0,1:T(8,128)(2,1)}) %all-gather.2.cloned.1.call-update) | async-done | bytes 1572880 | tf_op jit(solution)/shard_map/all_gather | solution.py:76
  62.8 1.5 %fusion.28 = (bf16[1,4,128,384]{3,2,0,1:T(8,128)(2,1)S(1)}, bf16[1,4,128,384]{3,2,0,1:T(8,128)(2,1)S(1)}, bf16[1,4,128,384]{3,2,0,1:T(8,128)(2,1)S(1)}, bf16[1,4,128,384]{3,2,0,1:T(8,128)(2,1)S(1)}) fusion(bf16[4,4,128,384]{3,2,0,1:T(8,128)(2,1)} %all-gather.2.cloned.1.call-done), kind=kLoop, calls=%fused_computation.51 | loop fusion | bytes 3145728 | tf_op jit(solution)/shard_map/slice | solution.py:78
  64.4 0.3 copy.64
  64.7 0.3 copy.70
  64.9 0.3 copy.67
  65.2 0.3 copy.73
  65.4 6.0 %convolution_bitcast_fusion.3 = f32[32,1,128,128]{2,0,3,1:T(8,128)S(1)} fusion(bf16[4,32,256]{1,0,2:T(4,128)(2,1)S(1)} %copy.66, bf16[1,4,128,384]{2,1,3,0:T(4,128)(2,1)S(1)} %copy.64), kind=kOutput, calls=%fused_computation.14 | convolution fusion | flops 1073741824 | bytes 2555904 | tf_op jit(solution)/shard_map/conv_general_dilated | solution.py:41
  71.4 6.0 %convolution_bitcast_fusion.1 = f32[32,1,128,128]{2,0,3,1:T(8,128)S(1)} fusion(bf16[4,32,256]{1,0,2:T(4,128)(2,1)S(1)} %copy.72, bf16[1,4,128,384]{2,1,3,0:T(4,128)(2,1)S(1)} %copy.70), kind=kOutput, calls=%fused_computation.12 | convolution fusion | flops 1073741824 | bytes 2555904 | tf_op jit(solution)/shard_map/conv_general_dilated | solution.py:41
  77.4 6.2 %convolution_bitcast_fusion.2 = f32[32,1,128,128]{2,0,3,1:T(8,128)S(1)} fusion(bf16[4,32,256]{1,0,2:T(4,128)(2,1)S(1)} %copy.69, bf16[1,4,128,384]{2,1,3,0:T(4,128)(2,1)S(1)} %copy.67), kind=kOutput, calls=%fused_computation.13 | convolution fusion | flops 1073741824 | bytes 2555904 | tf_op jit(solution)/shard_map/conv_general_dilated | solution.py:41
  83.6 6.0 %convolution_bitcast_fusion = f32[32,1,128,128]{2,0,3,1:T(8,128)S(1)} fusion(bf16[4,32,256]{1,0,2:T(4,128)(2,1)S(1)} %copy.75, bf16[1,4,128,384]{2,1,3,0:T(4,128)(2,1)S(1)} %copy.73), kind=kOutput, calls=%fused_computation.11 | convolution fusion | flops 1073741824 | bytes 2555904 | tf_op jit(solution)/shard_map/conv_general_dilated | solution.py:41
  89.6 4.1 %maximum_multiply_fusion = f32[32,4,128,128]{2,0,3,1:T(8,128)} fusion(f32[32,1,128,128]{2,0,3,1:T(8,128)S(1)} %convolution_bitcast_fusion, f32[32,1,128,128]{2,0,3,1:T(8,128)S(1)} %convolution_bitcast_fusion.1, f32[32,1,128,128]{2,0,3,1:T(8,128)S(1)} %convolution_bitcast_fusion.2, f32[32,1,128,128]{2,0,3,1:T(8,128)S(1)} %convolution_bitcast_fusion.3, ...), kind=kLoop, calls=%fused_computation.2 | loop fusion | flops 8388608 | bytes 16777232 | tf_op jit(solution)/shard_map/mul | solution.py:81
  93.8 9.9 %copy.62 = f32[32,4,128,128]{3,2,1,0:T(8,128)} copy(f32[32,4,128,128]{2,0,3,1:T(8,128)} %maximum_multiply_fusion) | data formatting | bytes 16777216 | tf_op jit(solution)/shard_map/mul | solution.py:81
  (29 shorter events, 1.0 us)
Async XLA Ops:
  6.5 1.0 copy-start
  6.5 2.6 %copy-start.1 = (bf16[1,40,16,512]{3,2,1,0:T(8,128)(2,1)S(1)}, bf16[1,40,16,512]{3,2,1,0:T(8,128)(2,1)}, u32[]{:S(2)}) copy-start(bf16[1,40,16,512]{3,2,1,0:T(8,128)(2,1)} %param.4) | copy-start | bytes 1966084
  6.5 56.3 %all-gather.2.cloned.1.call-start = ((), (), s32[]{:S(2)}) async-start(), calls=%async_computation.2 | async-start | bytes 1966080 | tf_op jit(solution)/shard_map/all_gather | solution.py:76
  40.0 5.7 %copy-start.2 = (s32[8,4,2]{0,2,1:T(2,128)S(1)}, s32[8,4,2]{0,2,1:T(2,128)}, u32[]{:S(2)}) copy-start(s32[8,4,2]{0,2,1:T(2,128)} %param.5) | copy-start | bytes 772
  42.0 14.4 %all-to-all-start.1 = ((bf16[4,1,128,384]{3,0,1,2:T(4,128)(2,1)}), bf16[4,1,128,384]{3,0,1,2:T(4,128)(2,1)S(1)}, u32[]{:S(2)}, u32[]{:S(2)}) async-start(bf16[4,1,128,384]{3,0,1,2:T(4,128)(2,1)} %copy.49), calls=%async_computation.1 | async-start | bytes 786432 | tf_op jit(solution)/shard_map/all_to_all | solution.py:74
Sparse Core Ops, SparseCore 0:
  41.1 21.6 all-gather.1
where the time goes:
time: 111 us
  blocking collectives  27.2 us (25%)
  matrix products  25.7 us (23%)
  local copies, waits for them, and re-layouts  18.7 us (17%)
  waiting for transfers between devices  15.2 us (14%)
  between operations  14.3 us (13%)
  other arithmetic  5.71 us (5%)
  starting transfers between devices  3.64 us (3%)
    all_to_all x1, blocking collectives, body(): lax.all_to_all(outgoing, 'pairs', split_axis=0, concat_axis=2, tiled=True)  27.2 us
    conv_general_dilated x4, matrix products, correlate(): lax.conv_general_dilated(source, kernel, (1,), 'VALID', dimension_numbers...  24.2 us
    all_to_all x1, waiting for transfers between devices, body(): lax.all_to_all(firsts[:, None], 'win', split_axis=2, concat_axis=1, tiled...  10.6 us
    mul x1, local copies, waits for them, and re-layouts, body(): return summed * scale * tile_valid[None, :, None, None]  9.9 us
    all_gather x1, waiting for transfers between devices, body(): piece = lax.all_gather(seconds[:, None], 'win', axis=1, tiled=True)  4.56 us
    mul x2, other arithmetic, body(): return summed * scale * tile_valid[None, :, None, None]  4.14 us
    all_to_all x1, starting transfers between devices, body(): lax.all_to_all(firsts[:, None], 'win', split_axis=2, concat_axis=1, tiled...  3.64 us
  transfers between devices with their start and end apart: 2, of which 2 were waited for; matrix products, arithmetic and copies ran while one was open for 3% of the time, Pallas kernels for 0%

commit v1 on v0

v1 whole, which is shorter than its diff:
```python
import functools
import math

import jax
import jax.numpy as jnp
from jax import lax
from jax.experimental import pallas as pl
from jax.experimental.pallas import tpu as pltpu
from jax.sharding import PartitionSpec as P

LAGS = 128
HALF = LAGS // 2
EPS = 1e-06
STEP = 16
GROUPS = ((0, 1, 2, 3), (4, 5, 6, 7))


def whiten_kernel(pairs_ref, slot_ref, offset_ref, raw_ref, *refs):
    outs, (full, lead) = refs[:-2], refs[-2:]
    _, slots, rows, rec = raw_ref.shape
    seg = rec - LAGS
    samples = seg - LAGS
    tiles = pairs_ref.shape[1]
    owner = lax.axis_index("pairs")
    band = (
        jnp.abs(
            lax.broadcasted_iota(jnp.int32, (seg, seg), 0)
            - lax.broadcasted_iota(jnp.int32, (seg, seg), 1)
        )
        <= HALF
    ).astype(jnp.bfloat16)
    position = lax.broadcasted_iota(jnp.int32, (1, seg), 1)
    tally = jnp.minimum(position, HALF) + jnp.minimum(seg - 1 - position, HALF) + 1
    inverse = 1.0 / tally.astype(jnp.float32)
    turn = lax.rem(rec - offset_ref[0], rec)
    chunk = 8

    def step(i, _):
        start = pl.multiple_of(i * chunk, chunk)
        raw = raw_ref[0, pl.ds(start, chunk)].reshape(chunk * rows, rec)
        signal = pltpu.roll(raw.astype(jnp.float32), turn, 1)[:, :seg]
        running = jnp.dot(
            jnp.abs(signal).astype(jnp.bfloat16), band, preferred_element_type=jnp.float32
        )
        whitened = signal / (running * inverse + EPS)
        full[pl.ds(start, chunk)] = whitened.astype(jnp.bfloat16).reshape(chunk, rows, seg)
        lead[pl.ds(start, chunk)] = (
            whitened[:, HALF : HALF + samples].astype(jnp.bfloat16).reshape(chunk, rows, samples)
        )
        return 0

    lax.fori_loop(0, slots // chunk, step, 0)
    for k, out in enumerate(outs):
        for t in range(tiles):
            first = slot_ref[jnp.maximum(pairs_ref[owner ^ k, t, 0], 0)]
            second = slot_ref[jnp.maximum(pairs_ref[owner ^ k, t, 1], 0)]
            out[t, :, :seg] = full[second]
            out[t, :, seg:] = lead[first]


def whiten_and_pack(raw_traces, tile_pairs, block_slot, win_offset):
    _, slots, rows, rec = raw_traces.shape
    owners, tiles, _ = tile_pairs.shape
    seg = rec - LAGS
    samples = seg - LAGS
    smem = pl.BlockSpec(memory_space=pltpu.SMEM)
    vmem = pl.BlockSpec(memory_space=pltpu.VMEM)
    return pl.pallas_call(
        whiten_kernel,
        in_specs=[smem, smem, smem, vmem],
        out_specs=[vmem] * owners,
        out_shape=[jax.ShapeDtypeStruct((tiles, rows, seg + samples), jnp.bfloat16)] * owners,
        scratch_shapes=[
            pltpu.VMEM((slots, rows, seg), jnp.bfloat16),
            pltpu.VMEM((slots, rows, samples), jnp.bfloat16),
        ],
        compiler_params=pltpu.CompilerParams(vmem_limit_bytes=24 << 20),
        name="whiten",
    )(tile_pairs, block_slot, win_offset, raw_traces)


def stack_kernel(place_ref, pairs_ref, *refs, windows, scale):
    n_in = windows * len(GROUPS)
    ins, o_ref, (block, lead, toeplitz, lagged, product) = refs[:n_in], refs[n_in], refs[n_in + 1 :]
    rows, _, chans, _ = o_ref.shape
    seg = lagged.shape[1]
    samples = seg - LAGS
    blocks = LAGS // STEP
    owner, share = place_ref[0], place_ref[1]
    tile = pl.program_id(0)
    wide = windows * samples
    n = block.shape[2]

    for w in range(windows):
        for g, group in enumerate(GROUPS):
            part = ins[g * windows + w]
            for i, k in enumerate(group):
                block[w, owner ^ k] = part[i, 0]
    for w in range(windows):
        lagged[w] = block[w, :, :, :seg].reshape(chans, seg).T
        for j in range(rows // n):
            lead[w, j * n : (j + 1) * n, :] = block[w, share * (rows // n) + j, :, seg:].astype(jnp.float32)

    def spread(c, _):
        tails = None
        at = pl.ds(pl.multiple_of(c * STEP, STEP), STEP)
        for w in range(windows):
            row = jnp.broadcast_to(lead[w, pl.ds(c, 1), :], (STEP, samples))
            row = jnp.concatenate([row, jnp.zeros((STEP, LAGS), jnp.float32)], 1)
            row = pltpu.roll(row, 0, 1, stride=1, stride_axis=0)
            toeplitz[at, w * samples : (w + 1) * samples] = row[:, :samples].astype(jnp.bfloat16)
            tail = row[:, samples:]
            if w:
                tail = pltpu.roll(tail, STEP * w, 1)
            tails = tail if tails is None else tails + tail
        toeplitz[at, wide:] = tails.astype(jnp.bfloat16)
        return 0

    lax.fori_loop(0, rows, spread, 0, unroll=4)

    for q in range(0, blocks, 2):
        halves = []
        for b in (q, q + 1):
            lo = STEP * b
            parts = [lagged[w, lo : lo + samples, :] for w in range(windows)]
            parts += [lagged[w, lo + samples : lo + samples + STEP, :] for w in range(windows)]
            parts.append(jnp.zeros((LAGS - windows * STEP, chans), jnp.bfloat16))
            halves.append(jnp.concatenate(parts, 0))
        r = jnp.dot(
            toeplitz[...], jnp.concatenate(halves, 1), preferred_element_type=jnp.float32
        )
        product[q] = r[:, :chans]
        product[q + 1] = r[:, chans:]

    factor = jnp.where(pairs_ref[owner, tile, 0] >= 0, scale, 0.0)

    def finish(c, _):
        at = pl.ds(pl.multiple_of(c * STEP, STEP), STEP)
        o_ref[c, 0] = product[:, at, :].reshape(LAGS, chans).T * factor
        return 0

    lax.fori_loop(0, rows, finish, 0, unroll=2)


def stack(place, tile_pairs, parts, windows, rows, chans, scale):
    _, tiles, n, width = parts[0].shape
    samples = (width - LAGS) // 2
    seg = samples + LAGS
    return pl.pallas_call(
        functools.partial(stack_kernel, windows=windows, scale=scale),
        grid=(tiles,),
        in_specs=[pl.BlockSpec(memory_space=pltpu.SMEM)] * 2
        + [pl.BlockSpec((p.shape[0], 1, n, width), lambda t: (0, t, 0, 0)) for p in parts],
        out_specs=pl.BlockSpec((rows, 1, chans, LAGS), lambda t: (0, t, 0, 0)),
        out_shape=jax.ShapeDtypeStruct((rows, tiles, chans, LAGS), jnp.float32),
        scratch_shapes=[
            pltpu.VMEM((windows, chans // n, n, width), jnp.bfloat16),
            pltpu.VMEM((windows, rows, samples), jnp.float32),
            pltpu.VMEM((rows * STEP, windows * samples + LAGS), jnp.bfloat16),
            pltpu.VMEM((windows, seg, chans), jnp.bfloat16),
            pltpu.VMEM((LAGS // STEP, rows * STEP, chans), jnp.float32),
        ],
        compiler_params=pltpu.CompilerParams(vmem_limit_bytes=40 << 20),
        name="stack",
    )(place, tile_pairs, *parts)


def body(raw_traces, tile_pairs, block_slot, win_offset):
    owners = lax.axis_size("pairs")
    windows = lax.axis_size("win")
    rows, rec = raw_traces.shape[2:]
    chans = rows * owners
    samples = rec - 2 * LAGS
    units = whiten_and_pack(raw_traces, tile_pairs, block_slot, win_offset)

    def swap(x, axis, size, k):
        return lax.ppermute(x, axis, [(i, i ^ k) for i in range(size)])

    units = [u if k == 0 else swap(u, "pairs", owners, k) for k, u in enumerate(units)]
    parts = []
    for group in GROUPS:
        held = jnp.stack([units[k] for k in group])
        other = swap(held, "win", windows, 2)
        parts += [held, other, swap(held, "win", windows, 1), swap(other, "win", windows, 1)]
    scale = 1.0 / math.sqrt(windows * samples)
    place = jnp.stack([lax.axis_index("pairs"), lax.axis_index("win")]).astype(jnp.int32)
    return stack(place, tile_pairs, parts, windows, chans // windows, chans, scale)


def plain_whiten(signal):
    length = signal.shape[-1]
    seg_count = length // LAGS
    magnitude = jnp.abs(signal).reshape(signal.shape[:-1] + (seg_count, LAGS))
    padded = jnp.pad(magnitude, [(0, 0)] * (magnitude.ndim - 2) + [(1, 1), (0, 0)])
    windows = jnp.concatenate([padded[..., :-2, :], padded[..., 1:-1, :], padded[..., 2:, :]], -1)
    rowpos = jnp.arange(3 * LAGS)[:, None]
    colpos = jnp.arange(LAGS)[None, :]
    band_matrix = (jnp.abs(rowpos - LAGS - colpos) <= HALF).astype(jnp.float32)
    totals = jnp.einsum(
        "...ni,ij->...nj", windows, band_matrix, precision=lax.Precision.HIGHEST
    ).reshape(signal.shape)
    position = jnp.arange(length)
    tally = (jnp.minimum(position, HALF) + jnp.minimum(length - 1 - position, HALF) + 1).astype(
        jnp.float32
    )
    return (signal / (totals / tally + EPS)).astype(jnp.bfloat16)


def plain_correlate(leading_blocks, trailing_blocks):
    seg_len = leading_blocks.shape[-1]
    samples = seg_len - LAGS
    kernel = jnp.transpose(leading_blocks[..., HALF : HALF + samples], (1, 0, 2))
    source = jnp.transpose(trailing_blocks[..., : seg_len - 1], (1, 0, 2))
    return lax.conv_general_dilated(
        source,
        kernel,
        (1,),
        "VALID",
        dimension_numbers=("NCH", "OIH", "CNH"),
        preferred_element_type=jnp.float32,
    )


def plain_body(raw_traces, tile_pairs, block_slot, win_offset):
    owner_index = lax.axis_index("pairs")
    pair_count = lax.axis_size("pairs")
    win_count = lax.axis_size("win")
    local_channels = raw_traces.shape[2]
    channels = local_channels * pair_count
    seg_len = raw_traces.shape[3] - LAGS
    samples = seg_len - LAGS
    tile_count = tile_pairs.shape[1]
    segment = lax.dynamic_slice_in_dim(raw_traces[0], win_offset[0], seg_len, 2).astype(jnp.float32)
    whitened = plain_whiten(segment)
    wanted = tile_pairs.reshape(pair_count, 2 * tile_count)
    slot_index = block_slot[jnp.maximum(wanted, 0)]
    outgoing = jnp.take(whitened, slot_index.reshape(-1), axis=0).reshape(
        pair_count, 2 * tile_count, local_channels, seg_len
    )
    incoming = lax.all_to_all(outgoing, "pairs", split_axis=0, concat_axis=2, tiled=True)
    blocks = incoming[0].reshape(tile_count, 2, channels, seg_len)
    own_tiles = lax.dynamic_index_in_dim(tile_pairs, owner_index, 0, keepdims=False)
    tile_valid = (own_tiles[:, 0] >= 0).astype(jnp.float32)
    firsts = blocks[:, 0]
    seconds = blocks[:, 1]
    spread_rows = lax.all_to_all(firsts[:, None], "win", split_axis=2, concat_axis=1, tiled=True)
    piece = lax.all_gather(seconds[:, None], "win", axis=1, tiled=True)
    summed = jnp.stack(
        [plain_correlate(spread_rows[tile], piece[tile]) for tile in range(tile_count)], 1
    )
    scale = 1.0 / math.sqrt(win_count * samples)
    return summed * scale * tile_valid[None, :, None, None]


def solution(mesh):
    regular = mesh.shape["pairs"] == 8 and mesh.shape["win"] == 4
    return jax.shard_map(
        body if regular else plain_body,
        mesh=mesh,
        in_specs=(P("win", None, "pairs", None), P(), P(), P("win")),
        out_specs=P("win", "pairs", None, None),
        check_vma=False,
    )
```

time: 111 us -> 65.9 us (0.59)
  the two profiles are of different devices: /device:TPU:0 before, /device:TPU:17 now
where the time goes in v1:
time: 65.9 us; the launch traced here: 65.7 us
  Pallas kernels  24.8 us (38%)
  starting transfers between devices  24.6 us (37%)
  waiting for transfers between devices  12.9 us (20%)
  local copies, waits for them, and re-layouts  2.53 us (4%)
  between operations  0.7 us (1%)
    ppermute x13, starting transfers between devices, swap(): return lax.ppermute(x, axis, [(i, i ^ k) for i in range(size)])  24.6 us
    pallas_call x1, Pallas kernels, stack(): pl.pallas_call(functools.partial(stack_kernel, windows=windows, scale=sca...  21.8 us
    ppermute x13, waiting for transfers between devices, swap(): return lax.ppermute(x, axis, [(i, i ^ k) for i in range(size)])  12.9 us
    pallas_call x1, Pallas kernels, whiten_and_pack(): pl.pallas_call(whiten_kernel, in_specs=[smem, smem, smem, vmem], out_spec...  2.94 us
    unnamed x5, local copies, waits for them, and re-layouts  2.53 us
  transfers between devices with their start and end apart: 13, of which 4 were waited for; matrix products, arithmetic and copies ran while one was open for 0% of the time, Pallas kernels for 0%

profile of v1, /device:TPU:17, one launch (start us, length us, event | category | flops | bytes accessed | tf_op | source)
XLA Modules:
  0.0 65.7 jit_solution(1528312465917281637)
XLA Ops:
  0.7 0.8 %copy.6.pairs_ref = s32[8,4,2]{2,1,0:T(4,128)S(1)} copy(s32[8,4,2]{0,2,1:T(2,128)} %param.5) | data formatting | bytes 512 | tf_op args[1]
  1.4 1.1 %copy-done = bf16[1,40,16,512]{3,2,1,0:T(8,128)(2,1)S(1)} copy-done((bf16[1,40,16,512]{3,2,1,0:T(8,128)(2,1)S(1)}, bf16[1,40,16,512]{3,2,1,0:T(8,128)(2,1)}, u32[]{:S(2)}) %copy-start) | copy-done | bytes 655384
  2.5 0.7 copy-done.1
  3.2 2.9 %whiten.1 = (bf16[4,16,640]{2,1,0:T(8,128)(2,1)S(1)}, bf16[4,16,640]{2,1,0:T(8,128)(2,1)S(1)}, bf16[4,16,640]{2,1,0:T(8,128)(2,1)S(1)}, bf16[4,16,640]{2,1,0:T(8...) custom-call(s32[8,4,2]{2,1,0:T(4,128)S(1)} %copy.6.pairs_ref, ...), custom_call_target="tpu_custom_call" | custom-call | tf_op jit(solution)/shard_map/whiten/pallas_call | solution.py:68
  6.1 0.1 collective-permute-start.6
  6.2 3.3 %collective-permute-start.7 = (bf16[4,16,640]{2,1,0:T(8,128)(2,1)S(1)}, bf16[4,16,640]{2,1,0:T(8,128)(2,1)S(1)}, u32[]{:S(2)}, u32[]{:S(2)}) collective-permute-start(bf16[4,16,640]{2,1,0:T(8,128)(2,1)S(1)} %get-tuple-element.18), channel_id=1, source_target_pairs={{0,20},{4,16},{8,28},{12,24},{16,4},{20,0},{24,12},{28,8},{1,21},{... | collective-permute-start | bytes 245768 | tf_op jit(solution)/shard_map/ppermute | solution.py:177
  9.5 0.2 collective-permute-start.8
  9.7 1.2 %collective-permute-start.9 = (bf16[4,16,640]{2,1,0:T(8,128)(2,1)S(1)}, bf16[4,16,640]{2,1,0:T(8,128)(2,1)S(1)}, u32[]{:S(2)}, u32[]{:S(2)}) collective-permute-start(bf16[4,16,640]{2,1,0:T(8,128)(2,1)S(1)} %get-tuple-element.20), channel_id=1, source_target_pairs={{0,28},{4,24},{8,20},{12,16},{16,12},{20,8},{24,4},{28,0},{1,29},{... | collective-permute-start | bytes 245768 | tf_op jit(solution)/shard_map/ppermute | solution.py:177
  10.9 1.2 %collective-permute-start = (bf16[4,16,640]{2,1,0:T(8,128)(2,1)S(1)}, bf16[4,16,640]{2,1,0:T(8,128)(2,1)S(1)}, u32[]{:S(2)}, u32[]{:S(2)}) collective-permute-start(bf16[4,16,640]{2,1,0:T(8,128)(2,1)S(1)} %get-tuple-element.14), channel_id=1, source_target_pairs={{0,4},{4,0},{8,12},{12,8},{16,20},{20,16},{24,28},{28,24},{1,5},{5... | collective-permute-start | bytes 245768 | tf_op jit(solution)/shard_map/ppermute | solution.py:177
  12.1 0.0 collective-permute-done.6
  12.1 7.5 %collective-permute-start.1 = (bf16[4,16,640]{2,1,0:T(8,128)(2,1)S(1)}, bf16[4,16,640]{2,1,0:T(8,128)(2,1)S(1)}, u32[]{:S(2)}, u32[]{:S(2)}) collective-permute-start(bf16[4,16,640]{2,1,0:T(8,128)(2,1)S(1)} %get-tuple-element.15), channel_id=1, source_target_pairs={{0,8},{4,12},{8,0},{12,4},{16,24},{20,28},{24,16},{28,20},{1,9},{5... | collective-permute-start | bytes 245768 | tf_op jit(solution)/shard_map/ppermute | solution.py:177
  19.6 0.0 collective-permute-done.7
  19.6 2.7 %collective-permute-start.2 = (bf16[4,16,640]{2,1,0:T(8,128)(2,1)S(1)}, bf16[4,16,640]{2,1,0:T(8,128)(2,1)S(1)}, u32[]{:S(2)}, u32[]{:S(2)}) collective-permute-start(bf16[4,16,640]{2,1,0:T(8,128)(2,1)S(1)} %get-tuple-element.16), channel_id=1, source_target_pairs={{0,12},{4,8},{8,4},{12,0},{16,28},{20,24},{24,20},{28,16},{1,13},{... | collective-permute-start | bytes 245768 | tf_op jit(solution)/shard_map/ppermute | solution.py:177
  22.3 0.0 collective-permute-done.8
  22.3 3.1 %collective-permute-done.9 = bf16[4,16,640]{2,1,0:T(8,128)(2,1)S(1)} collective-permute-done((bf16[4,16,640]{2,1,0:T(8,128)(2,1)S(1)}, bf16[4,16,640]{2,1,0:T(8,128)(2,1)S(1)}, u32[]{:S(2)}, u32[]{:S(2)}) %collective-permute-start.9) | collective-permute-done | bytes 81952 | tf_op jit(solution)/shard_map/ppermute | solution.py:177
  25.4 0.1 pad_maximum_fusion.1.refs_4_
  25.4 1.3 %collective-permute-start.10 = (bf16[4,4,16,640]{3,2,1,0:T(8,128)(2,1)S(1)}, bf16[4,4,16,640]{3,2,1,0:T(8,128)(2,1)S(1)}, u32[]{:S(2)}, u32[]{:S(2)}) collective-permute-start(bf16[4,4,16,640]{3,2,1,0:T(8,128)(2,1)S(1)} %pad_maximum_fusion.1.refs_4_), channel_id=1, source_target_pairs={{0,2},{1,3},{2,0},{3,1},{4,6},{5,7},{6,4},{7,5},{8,10},{9,11},{10,... | collective-permute-start | bytes 983048 | tf_op jit(solution)/shard_map/ppermute | solution.py:177
  26.7 0.0 collective-permute-done
  26.7 0.0 collective-permute-done.1
  26.7 0.0 collective-permute-done.2
  26.7 0.1 pad_maximum_fusion.refs_0_
  26.8 0.3 collective-permute-start.3
  27.1 1.5 %collective-permute-start.11 = (bf16[4,4,16,640]{3,2,1,0:T(8,128)(2,1)S(1)}, bf16[4,4,16,640]{3,2,1,0:T(8,128)(2,1)S(1)}, u32[]{:S(2)}, u32[]{:S(2)}) collective-permute-start(bf16[4,4,16,640]{3,2,1,0:T(8,128)(2,1)S(1)} %pad_maximum_fusion.1.refs_4_), channel_id=1, source_target_pairs={{0,1},{1,0},{2,3},{3,2},{4,5},{5,4},{6,7},{7,6},{8,9},{9,8},{10,11... | collective-permute-start | bytes 983048 | tf_op jit(solution)/shard_map/ppermute | solution.py:177
  28.6 0.0 collective-permute-start.4
  28.6 5.1 %collective-permute-done.10.refs_5_ = bf16[4,4,16,640]{3,2,1,0:T(8,128)(2,1)S(1)} collective-permute-done((bf16[4,4,16,640]{3,2,1,0:T(8,128)(2,1)S(1)}, bf16[4,4,16,640]{3,2,1,0:T(8,128)(2,1)S(1)}, u32[]{:S(2)}, u32[]{:S(2)}) %collective-permute-start.10) | collective-permute-done | bytes 327712 | tf_op jit(solution)/shard_map/ppermute | solution.py:177
  33.7 3.4 %collective-permute-start.12 = (bf16[4,4,16,640]{3,2,1,0:T(8,128)(2,1)S(1)}, bf16[4,4,16,640]{3,2,1,0:T(8,128)(2,1)S(1)}, u32[]{:S(2)}, u32[]{:S(2)}) collective-permute-start(bf16[4,4,16,640]{3,2,1,0:T(8,128)(2,1)S(1)} %collective-permute-done.10.refs_5_), channel_id=1, source_target_pairs={{0,1},{1,0},{2,3},{3,2},{4,5},{5,4},{6,7},{7,6},{8,9},{9,8},{10,11... | collective-permute-start | bytes 983048 | tf_op jit(solution)/shard_map/ppermute | solution.py:177
  37.1 3.6 %collective-permute-done.3.refs_1_ = bf16[4,4,16,640]{3,2,1,0:T(8,128)(2,1)S(1)} collective-permute-done((bf16[4,4,16,640]{3,2,1,0:T(8,128)(2,1)S(1)}, bf16[4,4,16,640]{3,2,1,0:T(8,128)(2,1)S(1)}, u32[]{:S(2)}, u32[]{:S(2)}) %collective-permute-start.3) | collective-permute-done | bytes 327712 | tf_op jit(solution)/shard_map/ppermute | solution.py:177
  40.7 1.9 %collective-permute-start.5 = (bf16[4,4,16,640]{3,2,1,0:T(8,128)(2,1)S(1)}, bf16[4,4,16,640]{3,2,1,0:T(8,128)(2,1)S(1)}, u32[]{:S(2)}, u32[]{:S(2)}) collective-permute-start(bf16[4,4,16,640]{3,2,1,0:T(8,128)(2,1)S(1)} %collective-permute-done.3.refs_1_), channel_id=1, source_target_pairs={{0,1},{1,0},{2,3},{3,2},{4,5},{5,4},{6,7},{7,6},{8,9},{9,8},{10,11... | collective-permute-start | bytes 983048 | tf_op jit(solution)/shard_map/ppermute | solution.py:177
  42.6 0.1 pad_add_fusion.place_ref
  42.7 0.0 collective-permute-done.11.refs_6_
  42.7 1.2 %collective-permute-done.5.refs_3_ = bf16[4,4,16,640]{3,2,1,0:T(8,128)(2,1)S(1)} collective-permute-done((bf16[4,4,16,640]{3,2,1,0:T(8,128)(2,1)S(1)}, bf16[4,4,16,640]{3,2,1,0:T(8,128)(2,1)S(1)}, u32[]{:S(2)}, u32[]{:S(2)}) %collective-permute-start.5) | collective-permute-done | bytes 327712 | tf_op jit(solution)/shard_map/ppermute | solution.py:177
  43.9 21.8 %stack.53 = f32[32,4,128,128]{3,2,1,0:T(8,128)} custom-call(s32[2]{0:T(128)S(1)} %pad_add_fusion.place_ref, s32[8,4,2]{2,1,0:T(4,128)S(1)} %copy.6.pairs_ref, bf16[4,4,16,640]{3,2,1,0:T(8,128)(2,1)S(1)} %pad_maximum_fusion.refs_0_, bf16[4,4,16,640]{3,2,1,0:T(8,128)(2,1)S(1)} %collective-permute-done.3.refs_1_, ...), custom_call_target="tpu_custom_call" | custom-call | tf_op jit(solution)/shard_map/stack/pallas_call | solution.py:149
  (4 shorter events, 0.0 us)
Async XLA Ops:
  1.4 1.1 %copy-start = (bf16[1,40,16,512]{3,2,1,0:T(8,128)(2,1)S(1)}, bf16[1,40,16,512]{3,2,1,0:T(8,128)(2,1)}, u32[]{:S(2)}) copy-start(bf16[1,40,16,512]{3,2,1,0:T(8,128)(2,1)} %raw_ref.1) | copy-start | bytes 1966084
  2.5 0.7 copy-start.1
  6.1 6.0 %collective-permute-start.6 = (bf16[4,16,640]{2,1,0:T(8,128)(2,1)S(1)}, bf16[4,16,640]{2,1,0:T(8,128)(2,1)S(1)}, u32[]{:S(2)}, u32[]{:S(2)}) collective-permute-start(bf16[4,16,640]{2,1,0:T(8,128)(2,1)S(1)} %get-tuple-element.17), channel_id=1, source_target_pairs={{0,16},{4,20},{8,24},{12,28},{16,0},{20,4},{24,8},{28,12},{1,17},{... | collective-permute-start | bytes 245768 | tf_op jit(solution)/shard_map/ppermute | solution.py:177
  6.2 13.4 %collective-permute-start.7 = (bf16[4,16,640]{2,1,0:T(8,128)(2,1)S(1)}, bf16[4,16,640]{2,1,0:T(8,128)(2,1)S(1)}, u32[]{:S(2)}, u32[]{:S(2)}) collective-permute-start(bf16[4,16,640]{2,1,0:T(8,128)(2,1)S(1)} %get-tuple-element.18), channel_id=1, source_target_pairs={{0,20},{4,16},{8,28},{12,24},{16,4},{20,0},{24,12},{28,8},{1,21},{... | collective-permute-start | bytes 245768 | tf_op jit(solution)/shard_map/ppermute | solution.py:177
  9.5 12.8 %collective-permute-start.8 = (bf16[4,16,640]{2,1,0:T(8,128)(2,1)S(1)}, bf16[4,16,640]{2,1,0:T(8,128)(2,1)S(1)}, u32[]{:S(2)}, u32[]{:S(2)}) collective-permute-start(bf16[4,16,640]{2,1,0:T(8,128)(2,1)S(1)} %get-tuple-element.19), channel_id=1, source_target_pairs={{0,24},{4,28},{8,16},{12,20},{16,8},{20,12},{24,0},{28,4},{1,25},{... | collective-permute-start | bytes 245768 | tf_op jit(solution)/shard_map/ppermute | solution.py:177
  9.7 15.7 %collective-permute-start.9 = (bf16[4,16,640]{2,1,0:T(8,128)(2,1)S(1)}, bf16[4,16,640]{2,1,0:T(8,128)(2,1)S(1)}, u32[]{:S(2)}, u32[]{:S(2)}) collective-permute-start(bf16[4,16,640]{2,1,0:T(8,128)(2,1)S(1)} %get-tuple-element.20), channel_id=1, source_target_pairs={{0,28},{4,24},{8,20},{12,16},{16,12},{20,8},{24,4},{28,0},{1,29},{... | collective-permute-start | bytes 245768 | tf_op jit(solution)/shard_map/ppermute | solution.py:177
  10.9 15.8 %collective-permute-start = (bf16[4,16,640]{2,1,0:T(8,128)(2,1)S(1)}, bf16[4,16,640]{2,1,0:T(8,128)(2,1)S(1)}, u32[]{:S(2)}, u32[]{:S(2)}) collective-permute-start(bf16[4,16,640]{2,1,0:T(8,128)(2,1)S(1)} %get-tuple-element.14), channel_id=1, source_target_pairs={{0,4},{4,0},{8,12},{12,8},{16,20},{20,16},{24,28},{28,24},{1,5},{5... | collective-permute-start | bytes 245768 | tf_op jit(solution)/shard_map/ppermute | solution.py:177
  12.1 14.6 %collective-permute-start.1 = (bf16[4,16,640]{2,1,0:T(8,128)(2,1)S(1)}, bf16[4,16,640]{2,1,0:T(8,128)(2,1)S(1)}, u32[]{:S(2)}, u32[]{:S(2)}) collective-permute-start(bf16[4,16,640]{2,1,0:T(8,128)(2,1)S(1)} %get-tuple-element.15), channel_id=1, source_target_pairs={{0,8},{4,12},{8,0},{12,4},{16,24},{20,28},{24,16},{28,20},{1,9},{5... | collective-permute-start | bytes 245768 | tf_op jit(solution)/shard_map/ppermute | solution.py:177
  19.6 7.1 %collective-permute-start.2 = (bf16[4,16,640]{2,1,0:T(8,128)(2,1)S(1)}, bf16[4,16,640]{2,1,0:T(8,128)(2,1)S(1)}, u32[]{:S(2)}, u32[]{:S(2)}) collective-permute-start(bf16[4,16,640]{2,1,0:T(8,128)(2,1)S(1)} %get-tuple-element.16), channel_id=1, source_target_pairs={{0,12},{4,8},{8,4},{12,0},{16,28},{20,24},{24,20},{28,16},{1,13},{... | collective-permute-start | bytes 245768 | tf_op jit(solution)/shard_map/ppermute | solution.py:177
  25.4 8.3 %collective-permute-start.10 = (bf16[4,4,16,640]{3,2,1,0:T(8,128)(2,1)S(1)}, bf16[4,4,16,640]{3,2,1,0:T(8,128)(2,1)S(1)}, u32[]{:S(2)}, u32[]{:S(2)}) collective-permute-start(bf16[4,4,16,640]{3,2,1,0:T(8,128)(2,1)S(1)} %pad_maximum_fusion.1.refs_4_), channel_id=1, source_target_pairs={{0,2},{1,3},{2,0},{3,1},{4,6},{5,7},{6,4},{7,5},{8,10},{9,11},{10,... | collective-permute-start | bytes 983048 | tf_op jit(solution)/shard_map/ppermute | solution.py:177
  26.8 13.9 %collective-permute-start.3 = (bf16[4,4,16,640]{3,2,1,0:T(8,128)(2,1)S(1)}, bf16[4,4,16,640]{3,2,1,0:T(8,128)(2,1)S(1)}, u32[]{:S(2)}, u32[]{:S(2)}) collective-permute-start(bf16[4,4,16,640]{3,2,1,0:T(8,128)(2,1)S(1)} %pad_maximum_fusion.refs_0_), channel_id=1, source_target_pairs={{0,2},{1,3},{2,0},{3,1},{4,6},{5,7},{6,4},{7,5},{8,10},{9,11},{10,... | collective-permute-start | bytes 983048 | tf_op jit(solution)/shard_map/ppermute | solution.py:177
  27.1 15.6 %collective-permute-start.11 = (bf16[4,4,16,640]{3,2,1,0:T(8,128)(2,1)S(1)}, bf16[4,4,16,640]{3,2,1,0:T(8,128)(2,1)S(1)}, u32[]{:S(2)}, u32[]{:S(2)}) collective-permute-start(bf16[4,4,16,640]{3,2,1,0:T(8,128)(2,1)S(1)} %pad_maximum_fusion.1.refs_4_), channel_id=1, source_target_pairs={{0,1},{1,0},{2,3},{3,2},{4,5},{5,4},{6,7},{7,6},{8,9},{9,8},{10,11... | collective-permute-start | bytes 983048 | tf_op jit(solution)/shard_map/ppermute | solution.py:177
  28.6 14.1 %collective-permute-start.4 = (bf16[4,4,16,640]{3,2,1,0:T(8,128)(2,1)S(1)}, bf16[4,4,16,640]{3,2,1,0:T(8,128)(2,1)S(1)}, u32[]{:S(2)}, u32[]{:S(2)}) collective-permute-start(bf16[4,4,16,640]{3,2,1,0:T(8,128)(2,1)S(1)} %pad_maximum_fusion.refs_0_), channel_id=1, source_target_pairs={{0,1},{1,0},{2,3},{3,2},{4,5},{5,4},{6,7},{7,6},{8,9},{9,8},{10,11... | collective-permute-start | bytes 983048 | tf_op jit(solution)/shard_map/ppermute | solution.py:177
  33.7 9.0 %collective-permute-start.12 = (bf16[4,4,16,640]{3,2,1,0:T(8,128)(2,1)S(1)}, bf16[4,4,16,640]{3,2,1,0:T(8,128)(2,1)S(1)}, u32[]{:S(2)}, u32[]{:S(2)}) collective-permute-start(bf16[4,4,16,640]{3,2,1,0:T(8,128)(2,1)S(1)} %collective-permute-done.10.refs_5_), channel_id=1, source_target_pairs={{0,1},{1,0},{2,3},{3,2},{4,5},{5,4},{6,7},{7,6},{8,9},{9,8},{10,11... | collective-permute-start | bytes 983048 | tf_op jit(solution)/shard_map/ppermute | solution.py:177
  40.7 3.2 %collective-permute-start.5 = (bf16[4,4,16,640]{3,2,1,0:T(8,128)(2,1)S(1)}, bf16[4,4,16,640]{3,2,1,0:T(8,128)(2,1)S(1)}, u32[]{:S(2)}, u32[]{:S(2)}) collective-permute-start(bf16[4,4,16,640]{3,2,1,0:T(8,128)(2,1)S(1)} %collective-permute-done.3.refs_1_), channel_id=1, source_target_pairs={{0,1},{1,0},{2,3},{3,2},{4,5},{5,4},{6,7},{7,6},{8,9},{9,8},{10,11... | collective-permute-start | bytes 983048 | tf_op jit(solution)/shard_map/ppermute | solution.py:177

commit v2 on v1

--- a/solution.py
+++ b/solution.py
@@ -12,7 +12,6 @@
 HALF = LAGS // 2
 EPS = 1e-06
 STEP = 16
-GROUPS = ((0, 1, 2, 3), (4, 5, 6, 7))
 
 
 def whiten_kernel(pairs_ref, slot_ref, offset_ref, raw_ref, *refs):
@@ -80,86 +79,135 @@
 
 
 def stack_kernel(place_ref, pairs_ref, *refs, windows, scale):
-    n_in = windows * len(GROUPS)
-    ins, o_ref, (block, lead, toeplitz, lagged, product) = refs[:n_in], refs[n_in], refs[n_in + 1 :]
-    rows, _, chans, _ = o_ref.shape
-    seg = lagged.shape[1]
+    n_in = 2 * windows
+    ins, out_ref = refs[:n_in], refs[n_in]
+    far, near = ins[:windows], ins[windows:]
+    lead, ends, *pairs_of, done = refs[n_in + 1 :]
+    toeplitz, lagged, product, staged = (pairs_of[i : i + 2] for i in range(0, 8, 2))
+    rows, tiles, chans, _ = out_ref.shape
+    half, _, n, _ = near[0].shape
+    seg = lagged[0].shape[1]
     samples = seg - LAGS
+    wide = windows * samples
     blocks = LAGS // STEP
+    rounds = blocks // 2
+    per = rows // rounds
     owner, share = place_ref[0], place_ref[1]
-    tile = pl.program_id(0)
-    wide = windows * samples
-    n = block.shape[2]
-
-    for w in range(windows):
-        for g, group in enumerate(GROUPS):
-            part = ins[g * windows + w]
-            for i, k in enumerate(group):
-                block[w, owner ^ k] = part[i, 0]
-    for w in range(windows):
-        lagged[w] = block[w, :, :, :seg].reshape(chans, seg).T
-        for j in range(rows // n):
-            lead[w, j * n : (j + 1) * n, :] = block[w, share * (rows // n) + j, :, seg:].astype(jnp.float32)
-
-    def spread(c, _):
-        tails = None
+    lane = lax.broadcasted_iota(jnp.int32, (STEP, LAGS), 1)
+    shift = lax.broadcasted_iota(jnp.int32, (STEP, LAGS), 0)
+    early = lane < shift
+    tail = (lax.rem(lane, STEP) < shift) & (lane < windows * STEP)
+
+    def unit(w, t, j, lanes):
+        k = owner ^ j
+        here = (k < half).astype(jnp.int32) * jnp.ones((n, 1), jnp.int32) > 0
+        at = k & (half - 1)
+        return jnp.where(here, near[w][at, t, :, lanes], far[w][at, t, :, lanes])
+
+    def prepare(t, s):
+        lanes = lax.broadcasted_iota(jnp.int32, (rows, LAGS), 1)
+        last = jnp.zeros((rows, LAGS), jnp.float32)
+        for w in range(windows):
+            second = [unit(w, t, j, slice(0, seg)) for j in range(2 * half)]
+            lagged[s][w] = jnp.concatenate(second, 0).T
+            first = [
+                unit(w, t, share * (rows // n) + j, slice(seg, seg + samples))
+                for j in range(rows // n)
+            ]
+            mine = jnp.concatenate(first, 0).astype(jnp.float32)
+            lead[w] = mine
+            at = (w - 1) * STEP % LAGS
+            last += jnp.where(
+                (lanes >= at) & (lanes < at + STEP),
+                pltpu.roll(mine[:, samples - LAGS :], w * STEP, 1) if w else mine[:, samples - LAGS :],
+                0.0,
+            )
+        ends[...] = last
+
+    def turned(row):
+        return pltpu.roll(jnp.broadcast_to(row, (STEP, LAGS)), 0, 1, stride=1, stride_axis=0)
+
+    def spread(c, s):
         at = pl.ds(pl.multiple_of(c * STEP, STEP), STEP)
         for w in range(windows):
-            row = jnp.broadcast_to(lead[w, pl.ds(c, 1), :], (STEP, samples))
-            row = jnp.concatenate([row, jnp.zeros((STEP, LAGS), jnp.float32)], 1)
-            row = pltpu.roll(row, 0, 1, stride=1, stride_axis=0)
-            toeplitz[at, w * samples : (w + 1) * samples] = row[:, :samples].astype(jnp.bfloat16)
-            tail = row[:, samples:]
-            if w:
-                tail = pltpu.roll(tail, STEP * w, 1)
-            tails = tail if tails is None else tails + tail
-        toeplitz[at, wide:] = tails.astype(jnp.bfloat16)
-        return 0
-
-    lax.fori_loop(0, rows, spread, 0, unroll=4)
-
-    for q in range(0, blocks, 2):
+            before = None
+            row = lead[w, pl.ds(c, 1), :]
+            for lo in range(0, samples, LAGS):
+                now = turned(row[:, lo : lo + LAGS])
+                fill = 0.0 if before is None else before
+                toeplitz[s][at, w * samples + lo : w * samples + lo + LAGS] = jnp.where(
+                    early, fill, now
+                ).astype(jnp.bfloat16)
+                before = now
+        toeplitz[s][at, wide:] = jnp.where(tail, turned(ends[pl.ds(c, 1), :]), 0.0).astype(jnp.bfloat16)
+
+    def multiply(q, s):
         halves = []
-        for b in (q, q + 1):
-            lo = STEP * b
-            parts = [lagged[w, lo : lo + samples, :] for w in range(windows)]
-            parts += [lagged[w, lo + samples : lo + samples + STEP, :] for w in range(windows)]
+        for b in range(2):
+            lo = (2 * q + b) * STEP
+            lo = lo if isinstance(lo, int) else pl.multiple_of(lo, STEP)
+            parts = [lagged[s][w, pl.ds(lo, samples), :] for w in range(windows)]
+            parts += [lagged[s][w, pl.ds(lo + samples, STEP), :] for w in range(windows)]
             parts.append(jnp.zeros((LAGS - windows * STEP, chans), jnp.bfloat16))
             halves.append(jnp.concatenate(parts, 0))
         r = jnp.dot(
-            toeplitz[...], jnp.concatenate(halves, 1), preferred_element_type=jnp.float32
+            toeplitz[s][...], jnp.concatenate(halves, 1), preferred_element_type=jnp.float32
         )
-        product[q] = r[:, :chans]
-        product[q + 1] = r[:, chans:]
-
-    factor = jnp.where(pairs_ref[owner, tile, 0] >= 0, scale, 0.0)
-
-    def finish(c, _):
+        product[s][2 * q] = r[:, :chans]
+        product[s][2 * q + 1] = r[:, chans:]
+
+    def finish(c, s, factor):
         at = pl.ds(pl.multiple_of(c * STEP, STEP), STEP)
-        o_ref[c, 0] = product[:, at, :].reshape(LAGS, chans).T * factor
-        return 0
-
-    lax.fori_loop(0, rows, finish, 0, unroll=2)
+        staged[s][c] = product[s][:, at, :].reshape(LAGS, chans).T * factor
+
+    def copy(t):
+        return pltpu.make_async_copy(staged[t % 2], out_ref.at[:, t], done.at[t % 2])
+
+    for t in range(-1, tiles + 1):
+        if t + 1 < tiles:
+            prepare(t + 1, (t + 1) % 2)
+        if t >= 1:
+            factor = jnp.where(pairs_ref[owner, t - 1, 0] >= 0, scale, 0.0)
+            if t >= 3:
+                copy(t - 3).wait()
+
+        def step(q, _):
+            if 0 <= t < tiles:
+                multiply(q, t % 2)
+            for i in range(per):
+                if t + 1 < tiles:
+                    spread(q * per + i, (t + 1) % 2)
+                if t >= 1:
+                    finish(q * per + i, (t - 1) % 2, factor)
+            return 0
+
+        lax.fori_loop(0, rounds, step, 0, unroll=True)
+        if t >= 1:
+            copy(t - 1).start()
+    for t in range(max(tiles - 2, 0), tiles):
+        copy(t).wait()
 
 
 def stack(place, tile_pairs, parts, windows, rows, chans, scale):
     _, tiles, n, width = parts[0].shape
     samples = (width - LAGS) // 2
     seg = samples + LAGS
+    smem = pl.BlockSpec(memory_space=pltpu.SMEM)
+    vmem = pl.BlockSpec(memory_space=pltpu.VMEM)
     return pl.pallas_call(
         functools.partial(stack_kernel, windows=windows, scale=scale),
-        grid=(tiles,),
-        in_specs=[pl.BlockSpec(memory_space=pltpu.SMEM)] * 2
-        + [pl.BlockSpec((p.shape[0], 1, n, width), lambda t: (0, t, 0, 0)) for p in parts],
-        out_specs=pl.BlockSpec((rows, 1, chans, LAGS), lambda t: (0, t, 0, 0)),
+        in_specs=[smem] * 2 + [vmem] * len(parts),
+        out_specs=pl.BlockSpec(memory_space=pl.ANY),
         out_shape=jax.ShapeDtypeStruct((rows, tiles, chans, LAGS), jnp.float32),
         scratch_shapes=[
-            pltpu.VMEM((windows, chans // n, n, width), jnp.bfloat16),
             pltpu.VMEM((windows, rows, samples), jnp.float32),
-            pltpu.VMEM((rows * STEP, windows * samples + LAGS), jnp.bfloat16),
-            pltpu.VMEM((windows, seg, chans), jnp.bfloat16),
-            pltpu.VMEM((LAGS // STEP, rows * STEP, chans), jnp.float32),
-        ],
+            pltpu.VMEM((rows, LAGS), jnp.float32),
+        ]
+        + [pltpu.VMEM((rows * STEP, windows * samples + LAGS), jnp.bfloat16)] * 2
+        + [pltpu.VMEM((windows, seg, chans), jnp.bfloat16)] * 2
+        + [pltpu.VMEM((LAGS // STEP, rows * STEP, chans), jnp.float32)] * 2
+        + [pltpu.VMEM((rows, chans, LAGS), jnp.float32)] * 2
+        + [pltpu.SemaphoreType.DMA((2,))],
         compiler_params=pltpu.CompilerParams(vmem_limit_bytes=40 << 20),
         name="stack",
     )(place, tile_pairs, *parts)
@@ -178,8 +226,8 @@
 
     units = [u if k == 0 else swap(u, "pairs", owners, k) for k, u in enumerate(units)]
     parts = []
-    for group in GROUPS:
-        held = jnp.stack([units[k] for k in group])
+    for low in (owners // 2, 0):
+        held = jnp.stack(units[low : low + owners // 2])
         other = swap(held, "win", windows, 2)
         parts += [held, other, swap(held, "win", windows, 1), swap(other, "win", windows, 1)]
     scale = 1.0 / math.sqrt(windows * samples)

time: 65.9 us -> 48.2 us (0.73)
  Pallas kernels: 24.8 us -> 12.2 us
  starting transfers between devices: 24.6 us -> 13.2 us
  waiting for transfers between devices: 12.9 us -> 19.2 us
    pallas_call x1, Pallas kernels: 21.8 us -> 9.27 us  [stack(): pl.pallas_call(functools.partial(stack_kernel, windows=windows, scale=sca...]
    ppermute x13, starting transfers between devices: 24.6 us -> 13.2 us  [swap(): return lax.ppermute(x, axis, [(i, i ^ k) for i in range(size)])]
    ppermute x13, waiting for transfers between devices: 12.9 us -> 19.2 us  [swap(): return lax.ppermute(x, axis, [(i, i ^ k) for i in range(size)])]
  transfers between devices with their start and end apart: 13 -> 13, of which waited for: 4 -> 5; matrix products, arithmetic and copies ran while one was open for 0% -> 0% of each run, Pallas kernels for 0% -> 0%
where the time goes in v2:
time: 48.2 us; the launch traced here: 48 us
  waiting for transfers between devices  19.2 us (40%)
  starting transfers between devices  13.2 us (27%)
  Pallas kernels  12.2 us (25%)
  local copies, waits for them, and re-layouts  2.53 us (5%)
  between operations  0.69 us (1%)
    ppermute x13, waiting for transfers between devices, swap(): return lax.ppermute(x, axis, [(i, i ^ k) for i in range(size)])  19.2 us
    ppermute x13, starting transfers between devices, swap(): return lax.ppermute(x, axis, [(i, i ^ k) for i in range(size)])  13.2 us
    pallas_call x1, Pallas kernels, stack(): pl.pallas_call(functools.partial(stack_kernel, windows=windows, scale=sca...  9.27 us
    pallas_call x1, Pallas kernels, whiten_and_pack(): pl.pallas_call(whiten_kernel, in_specs=[smem, smem, smem, vmem], out_spec...  2.94 us
    unnamed x5, local copies, waits for them, and re-layouts  2.53 us
  transfers between devices with their start and end apart: 13, of which 5 were waited for; matrix products, arithmetic and copies ran while one was open for 0% of the time, Pallas kernels for 0%

profile of v2, /device:TPU:17, one launch (start us, length us, event | category | flops | bytes accessed | tf_op | source)
XLA Modules:
  0.0 48.0 jit_solution(16814263447670330213)
XLA Ops:
  0.7 0.8 %copy.6.pairs_ref = s32[8,4,2]{2,1,0:T(4,128)S(1)} copy(s32[8,4,2]{0,2,1:T(2,128)} %param.5) | data formatting | bytes 512 | tf_op args[1]
  1.4 1.1 %copy-done = bf16[1,40,16,512]{3,2,1,0:T(8,128)(2,1)S(1)} copy-done((bf16[1,40,16,512]{3,2,1,0:T(8,128)(2,1)S(1)}, bf16[1,40,16,512]{3,2,1,0:T(8,128)(2,1)}, u32[]{:S(2)}) %copy-start) | copy-done | bytes 655384
  2.5 0.7 %copy-done.1 = s32[40]{0:T(128)S(1)} copy-done((s32[40]{0:T(128)S(1)}, s32[40]{0:T(128)}, u32[]{:S(2)}) %copy-start.1) | copy-done | bytes 184
  3.2 2.9 %whiten.1 = (bf16[4,16,640]{2,1,0:T(8,128)(2,1)S(1)}, bf16[4,16,640]{2,1,0:T(8,128)(2,1)S(1)}, bf16[4,16,640]{2,1,0:T(8,128)(2,1)S(1)}, bf16[4,16,640]{2,1,0:T(8...) custom-call(s32[8,4,2]{2,1,0:T(4,128)S(1)} %copy.6.pairs_ref, ...), custom_call_target="tpu_custom_call" | custom-call | tf_op jit(solution)/shard_map/whiten/pallas_call | solution.py:67
  6.1 1.3 %collective-permute-start.7 = (bf16[4,16,640]{2,1,0:T(8,128)(2,1)S(1)}, bf16[4,16,640]{2,1,0:T(8,128)(2,1)S(1)}, u32[]{:S(2)}, u32[]{:S(2)}) collective-permute-start(bf16[4,16,640]{2,1,0:T(8,128)(2,1)S(1)} %get-tuple-element.18), channel_id=1, source_target_pairs={{0,4},{4,0},{8,12},{12,8},{16,20},{20,16},{24,28},{28,24},{1,5},{5... | collective-permute-start | bytes 245768 | tf_op jit(solution)/shard_map/ppermute | solution.py:225
  7.4 1.3 %collective-permute-start.8 = (bf16[4,16,640]{2,1,0:T(8,128)(2,1)S(1)}, bf16[4,16,640]{2,1,0:T(8,128)(2,1)S(1)}, u32[]{:S(2)}, u32[]{:S(2)}) collective-permute-start(bf16[4,16,640]{2,1,0:T(8,128)(2,1)S(1)} %get-tuple-element.19), channel_id=1, source_target_pairs={{0,8},{4,12},{8,0},{12,4},{16,24},{20,28},{24,16},{28,20},{1,9},{5... | collective-permute-start | bytes 245768 | tf_op jit(solution)/shard_map/ppermute | solution.py:225
  8.7 0.1 collective-permute-start.9
  8.8 0.0 collective-permute-start
  8.8 3.3 %collective-permute-start.1 = (bf16[4,16,640]{2,1,0:T(8,128)(2,1)S(1)}, bf16[4,16,640]{2,1,0:T(8,128)(2,1)S(1)}, u32[]{:S(2)}, u32[]{:S(2)}) collective-permute-start(bf16[4,16,640]{2,1,0:T(8,128)(2,1)S(1)} %get-tuple-element.14), channel_id=1, source_target_pairs={{0,20},{4,16},{8,28},{12,24},{16,4},{20,0},{24,12},{28,8},{1,21},{... | collective-permute-start | bytes 245768 | tf_op jit(solution)/shard_map/ppermute | solution.py:225
  12.1 0.0 collective-permute-done.7
  12.1 0.2 collective-permute-start.2
  12.3 0.0 collective-permute-done.8
  12.3 1.3 %collective-permute-start.3 = (bf16[4,16,640]{2,1,0:T(8,128)(2,1)S(1)}, bf16[4,16,640]{2,1,0:T(8,128)(2,1)S(1)}, u32[]{:S(2)}, u32[]{:S(2)}) collective-permute-start(bf16[4,16,640]{2,1,0:T(8,128)(2,1)S(1)} %get-tuple-element.16), channel_id=1, source_target_pairs={{0,28},{4,24},{8,20},{12,16},{16,12},{20,8},{24,4},{28,0},{1,29},{... | collective-permute-start | bytes 245768 | tf_op jit(solution)/shard_map/ppermute | solution.py:225
  13.6 0.0 collective-permute-done.9
  13.6 0.1 pad_maximum_fusion.1.refs_4_
  13.6 1.3 %collective-permute-start.10 = (bf16[4,4,16,640]{3,2,1,0:T(8,128)(2,1)S(1)}, bf16[4,4,16,640]{3,2,1,0:T(8,128)(2,1)S(1)}, u32[]{:S(2)}, u32[]{:S(2)}) collective-permute-start(bf16[4,4,16,640]{3,2,1,0:T(8,128)(2,1)S(1)} %pad_maximum_fusion.1.refs_4_), channel_id=1, source_target_pairs={{0,2},{1,3},{2,0},{3,1},{4,6},{5,7},{6,4},{7,5},{8,10},{9,11},{10,... | collective-permute-start | bytes 983048 | tf_op jit(solution)/shard_map/ppermute | solution.py:225
  14.9 0.0 collective-permute-done
  15.0 0.7 %collective-permute-done.1 = bf16[4,16,640]{2,1,0:T(8,128)(2,1)S(1)} collective-permute-done((bf16[4,16,640]{2,1,0:T(8,128)(2,1)S(1)}, bf16[4,16,640]{2,1,0:T(8,128)(2,1)S(1)}, u32[]{:S(2)}, u32[]{:S(2)}) %collective-permute-start.1) | collective-permute-done | bytes 81952 | tf_op jit(solution)/shard_map/ppermute | solution.py:225
  15.6 7.8 %collective-permute-done.2 = bf16[4,16,640]{2,1,0:T(8,128)(2,1)S(1)} collective-permute-done((bf16[4,16,640]{2,1,0:T(8,128)(2,1)S(1)}, bf16[4,16,640]{2,1,0:T(8,128)(2,1)S(1)}, u32[]{:S(2)}, u32[]{:S(2)}) %collective-permute-start.2) | collective-permute-done | bytes 81952 | tf_op jit(solution)/shard_map/ppermute | solution.py:225
  23.4 3.7 %collective-permute-done.3 = bf16[4,16,640]{2,1,0:T(8,128)(2,1)S(1)} collective-permute-done((bf16[4,16,640]{2,1,0:T(8,128)(2,1)S(1)}, bf16[4,16,640]{2,1,0:T(8,128)(2,1)S(1)}, u32[]{:S(2)}, u32[]{:S(2)}) %collective-permute-start.3) | collective-permute-done | bytes 81952 | tf_op jit(solution)/shard_map/ppermute | solution.py:225
  27.2 0.1 pad_maximum_fusion.refs_0_
  27.2 1.3 %collective-permute-start.4 = (bf16[4,4,16,640]{3,2,1,0:T(8,128)(2,1)S(1)}, bf16[4,4,16,640]{3,2,1,0:T(8,128)(2,1)S(1)}, u32[]{:S(2)}, u32[]{:S(2)}) collective-permute-start(bf16[4,4,16,640]{3,2,1,0:T(8,128)(2,1)S(1)} %pad_maximum_fusion.refs_0_), channel_id=1, source_target_pairs={{0,2},{1,3},{2,0},{3,1},{4,6},{5,7},{6,4},{7,5},{8,10},{9,11},{10,... | collective-permute-start | bytes 983048 | tf_op jit(solution)/shard_map/ppermute | solution.py:225
  28.5 1.0 %collective-permute-start.11 = (bf16[4,4,16,640]{3,2,1,0:T(8,128)(2,1)S(1)}, bf16[4,4,16,640]{3,2,1,0:T(8,128)(2,1)S(1)}, u32[]{:S(2)}, u32[]{:S(2)}) collective-permute-start(bf16[4,4,16,640]{3,2,1,0:T(8,128)(2,1)S(1)} %pad_maximum_fusion.1.refs_4_), channel_id=1, source_target_pairs={{0,1},{1,0},{2,3},{3,2},{4,5},{5,4},{6,7},{7,6},{8,9},{9,8},{10,11... | collective-permute-start | bytes 983048 | tf_op jit(solution)/shard_map/ppermute | solution.py:225
  29.5 0.0 collective-permute-start.5
  29.6 0.0 collective-permute-done.10.refs_5_
  29.6 0.5 %collective-permute-start.12 = (bf16[4,4,16,640]{3,2,1,0:T(8,128)(2,1)S(1)}, bf16[4,4,16,640]{3,2,1,0:T(8,128)(2,1)S(1)}, u32[]{:S(2)}, u32[]{:S(2)}) collective-permute-start(bf16[4,4,16,640]{3,2,1,0:T(8,128)(2,1)S(1)} %collective-permute-done.10.refs_5_), channel_id=1, source_target_pairs={{0,1},{1,0},{2,3},{3,2},{4,5},{5,4},{6,7},{7,6},{8,9},{9,8},{10,11... | collective-permute-start | bytes 983048 | tf_op jit(solution)/shard_map/ppermute | solution.py:225
  30.1 5.8 %collective-permute-done.4.refs_1_ = bf16[4,4,16,640]{3,2,1,0:T(8,128)(2,1)S(1)} collective-permute-done((bf16[4,4,16,640]{3,2,1,0:T(8,128)(2,1)S(1)}, bf16[4,4,16,640]{3,2,1,0:T(8,128)(2,1)S(1)}, u32[]{:S(2)}, u32[]{:S(2)}) %collective-permute-start.4) | collective-permute-done | bytes 327712 | tf_op jit(solution)/shard_map/ppermute | solution.py:225
  35.8 1.6 %collective-permute-start.6 = (bf16[4,4,16,640]{3,2,1,0:T(8,128)(2,1)S(1)}, bf16[4,4,16,640]{3,2,1,0:T(8,128)(2,1)S(1)}, u32[]{:S(2)}, u32[]{:S(2)}) collective-permute-start(bf16[4,4,16,640]{3,2,1,0:T(8,128)(2,1)S(1)} %collective-permute-done.4.refs_1_), channel_id=1, source_target_pairs={{0,1},{1,0},{2,3},{3,2},{4,5},{5,4},{6,7},{7,6},{8,9},{9,8},{10,11... | collective-permute-start | bytes 983048 | tf_op jit(solution)/shard_map/ppermute | solution.py:225
  37.4 0.1 pad_add_fusion.place_ref
  37.5 0.0 collective-permute-done.11.refs_6_
  37.5 1.2 %collective-permute-done.6.refs_3_ = bf16[4,4,16,640]{3,2,1,0:T(8,128)(2,1)S(1)} collective-permute-done((bf16[4,4,16,640]{3,2,1,0:T(8,128)(2,1)S(1)}, bf16[4,4,16,640]{3,2,1,0:T(8,128)(2,1)S(1)}, u32[]{:S(2)}, u32[]{:S(2)}) %collective-permute-start.6) | collective-permute-done | bytes 327712 | tf_op jit(solution)/shard_map/ppermute | solution.py:225
  38.7 9.3 %stack.53 = f32[32,4,128,128]{3,2,1,0:T(8,128)} custom-call(s32[2]{0:T(128)S(1)} %pad_add_fusion.place_ref, s32[8,4,2]{2,1,0:T(4,128)S(1)} %copy.6.pairs_ref, bf16[4,4,16,640]{3,2,1,0:T(8,128)(2,1)S(1)} %pad_maximum_fusion.refs_0_, bf16[4,4,16,640]{3,2,1,0:T(8,128)(2,1)S(1)} %collective-permute-done.4.refs_1_, ...), custom_call_target="tpu_custom_call" | custom-call | tf_op jit(solution)/shard_map/stack/pallas_call | solution.py:197
  (4 shorter events, 0.0 us)
Async XLA Ops:
  1.4 1.1 %copy-start = (bf16[1,40,16,512]{3,2,1,0:T(8,128)(2,1)S(1)}, bf16[1,40,16,512]{3,2,1,0:T(8,128)(2,1)}, u32[]{:S(2)}) copy-start(bf16[1,40,16,512]{3,2,1,0:T(8,128)(2,1)} %raw_ref.1) | copy-start | bytes 1966084
  2.5 0.7 %copy-start.1 = (s32[40]{0:T(128)S(1)}, s32[40]{0:T(128)}, u32[]{:S(2)}) copy-start(s32[40]{0:T(128)} %slot_ref.1) | copy-start | bytes 484
  6.1 6.0 %collective-permute-start.7 = (bf16[4,16,640]{2,1,0:T(8,128)(2,1)S(1)}, bf16[4,16,640]{2,1,0:T(8,128)(2,1)S(1)}, u32[]{:S(2)}, u32[]{:S(2)}) collective-permute-start(bf16[4,16,640]{2,1,0:T(8,128)(2,1)S(1)} %get-tuple-element.18), channel_id=1, source_target_pairs={{0,4},{4,0},{8,12},{12,8},{16,20},{20,16},{24,28},{28,24},{1,5},{5... | collective-permute-start | bytes 245768 | tf_op jit(solution)/shard_map/ppermute | solution.py:225
  7.4 4.9 %collective-permute-start.8 = (bf16[4,16,640]{2,1,0:T(8,128)(2,1)S(1)}, bf16[4,16,640]{2,1,0:T(8,128)(2,1)S(1)}, u32[]{:S(2)}, u32[]{:S(2)}) collective-permute-start(bf16[4,16,640]{2,1,0:T(8,128)(2,1)S(1)} %get-tuple-element.19), channel_id=1, source_target_pairs={{0,8},{4,12},{8,0},{12,4},{16,24},{20,28},{24,16},{28,20},{1,9},{5... | collective-permute-start | bytes 245768 | tf_op jit(solution)/shard_map/ppermute | solution.py:225
  8.7 4.9 %collective-permute-start.9 = (bf16[4,16,640]{2,1,0:T(8,128)(2,1)S(1)}, bf16[4,16,640]{2,1,0:T(8,128)(2,1)S(1)}, u32[]{:S(2)}, u32[]{:S(2)}) collective-permute-start(bf16[4,16,640]{2,1,0:T(8,128)(2,1)S(1)} %get-tuple-element.20), channel_id=1, source_target_pairs={{0,12},{4,8},{8,4},{12,0},{16,28},{20,24},{24,20},{28,16},{1,13},{... | collective-permute-start | bytes 245768 | tf_op jit(solution)/shard_map/ppermute | solution.py:225
  8.8 6.1 %collective-permute-start = (bf16[4,16,640]{2,1,0:T(8,128)(2,1)S(1)}, bf16[4,16,640]{2,1,0:T(8,128)(2,1)S(1)}, u32[]{:S(2)}, u32[]{:S(2)}) collective-permute-start(bf16[4,16,640]{2,1,0:T(8,128)(2,1)S(1)} %get-tuple-element.13), channel_id=1, source_target_pairs={{0,16},{4,20},{8,24},{12,28},{16,0},{20,4},{24,8},{28,12},{1,17},{... | collective-permute-start | bytes 245768 | tf_op jit(solution)/shard_map/ppermute | solution.py:225
  8.8 6.8 %collective-permute-start.1 = (bf16[4,16,640]{2,1,0:T(8,128)(2,1)S(1)}, bf16[4,16,640]{2,1,0:T(8,128)(2,1)S(1)}, u32[]{:S(2)}, u32[]{:S(2)}) collective-permute-start(bf16[4,16,640]{2,1,0:T(8,128)(2,1)S(1)} %get-tuple-element.14), channel_id=1, source_target_pairs={{0,20},{4,16},{8,28},{12,24},{16,4},{20,0},{24,12},{28,8},{1,21},{... | collective-permute-start | bytes 245768 | tf_op jit(solution)/shard_map/ppermute | solution.py:225
  12.1 11.3 %collective-permute-start.2 = (bf16[4,16,640]{2,1,0:T(8,128)(2,1)S(1)}, bf16[4,16,640]{2,1,0:T(8,128)(2,1)S(1)}, u32[]{:S(2)}, u32[]{:S(2)}) collective-permute-start(bf16[4,16,640]{2,1,0:T(8,128)(2,1)S(1)} %get-tuple-element.15), channel_id=1, source_target_pairs={{0,24},{4,28},{8,16},{12,20},{16,8},{20,12},{24,0},{28,4},{1,25},{... | collective-permute-start | bytes 245768 | tf_op jit(solution)/shard_map/ppermute | solution.py:225
  12.3 14.9 %collective-permute-start.3 = (bf16[4,16,640]{2,1,0:T(8,128)(2,1)S(1)}, bf16[4,16,640]{2,1,0:T(8,128)(2,1)S(1)}, u32[]{:S(2)}, u32[]{:S(2)}) collective-permute-start(bf16[4,16,640]{2,1,0:T(8,128)(2,1)S(1)} %get-tuple-element.16), channel_id=1, source_target_pairs={{0,28},{4,24},{8,20},{12,16},{16,12},{20,8},{24,4},{28,0},{1,29},{... | collective-permute-start | bytes 245768 | tf_op jit(solution)/shard_map/ppermute | solution.py:225
  13.6 15.9 %collective-permute-start.10 = (bf16[4,4,16,640]{3,2,1,0:T(8,128)(2,1)S(1)}, bf16[4,4,16,640]{3,2,1,0:T(8,128)(2,1)S(1)}, u32[]{:S(2)}, u32[]{:S(2)}) collective-permute-start(bf16[4,4,16,640]{3,2,1,0:T(8,128)(2,1)S(1)} %pad_maximum_fusion.1.refs_4_), channel_id=1, source_target_pairs={{0,2},{1,3},{2,0},{3,1},{4,6},{5,7},{6,4},{7,5},{8,10},{9,11},{10,... | collective-permute-start | bytes 983048 | tf_op jit(solution)/shard_map/ppermute | solution.py:225
  27.2 8.6 %collective-permute-start.4 = (bf16[4,4,16,640]{3,2,1,0:T(8,128)(2,1)S(1)}, bf16[4,4,16,640]{3,2,1,0:T(8,128)(2,1)S(1)}, u32[]{:S(2)}, u32[]{:S(2)}) collective-permute-start(bf16[4,4,16,640]{3,2,1,0:T(8,128)(2,1)S(1)} %pad_maximum_fusion.refs_0_), channel_id=1, source_target_pairs={{0,2},{1,3},{2,0},{3,1},{4,6},{5,7},{6,4},{7,5},{8,10},{9,11},{10,... | collective-permute-start | bytes 983048 | tf_op jit(solution)/shard_map/ppermute | solution.py:225
  28.5 9.0 %collective-permute-start.11 = (bf16[4,4,16,640]{3,2,1,0:T(8,128)(2,1)S(1)}, bf16[4,4,16,640]{3,2,1,0:T(8,128)(2,1)S(1)}, u32[]{:S(2)}, u32[]{:S(2)}) collective-permute-start(bf16[4,4,16,640]{3,2,1,0:T(8,128)(2,1)S(1)} %pad_maximum_fusion.1.refs_4_), channel_id=1, source_target_pairs={{0,1},{1,0},{2,3},{3,2},{4,5},{5,4},{6,7},{7,6},{8,9},{9,8},{10,11... | collective-permute-start | bytes 983048 | tf_op jit(solution)/shard_map/ppermute | solution.py:225
  29.5 8.0 %collective-permute-start.5 = (bf16[4,4,16,640]{3,2,1,0:T(8,128)(2,1)S(1)}, bf16[4,4,16,640]{3,2,1,0:T(8,128)(2,1)S(1)}, u32[]{:S(2)}, u32[]{:S(2)}) collective-permute-start(bf16[4,4,16,640]{3,2,1,0:T(8,128)(2,1)S(1)} %pad_maximum_fusion.refs_0_), channel_id=1, source_target_pairs={{0,1},{1,0},{2,3},{3,2},{4,5},{5,4},{6,7},{7,6},{8,9},{9,8},{10,11... | collective-permute-start | bytes 983048 | tf_op jit(solution)/shard_map/ppermute | solution.py:225
  29.6 8.0 %collective-permute-start.12 = (bf16[4,4,16,640]{3,2,1,0:T(8,128)(2,1)S(1)}, bf16[4,4,16,640]{3,2,1,0:T(8,128)(2,1)S(1)}, u32[]{:S(2)}, u32[]{:S(2)}) collective-permute-start(bf16[4,4,16,640]{3,2,1,0:T(8,128)(2,1)S(1)} %collective-permute-done.10.refs_5_), channel_id=1, source_target_pairs={{0,1},{1,0},{2,3},{3,2},{4,5},{5,4},{6,7},{7,6},{8,9},{9,8},{10,11... | collective-permute-start | bytes 983048 | tf_op jit(solution)/shard_map/ppermute | solution.py:225
  35.8 2.9 %collective-permute-start.6 = (bf16[4,4,16,640]{3,2,1,0:T(8,128)(2,1)S(1)}, bf16[4,4,16,640]{3,2,1,0:T(8,128)(2,1)S(1)}, u32[]{:S(2)}, u32[]{:S(2)}) collective-permute-start(bf16[4,4,16,640]{3,2,1,0:T(8,128)(2,1)S(1)} %collective-permute-done.4.refs_1_), channel_id=1, source_target_pairs={{0,1},{1,0},{2,3},{3,2},{4,5},{5,4},{6,7},{7,6},{8,9},{9,8},{10,11... | collective-permute-start | bytes 983048 | tf_op jit(solution)/shard_map/ppermute | solution.py:225

commit v3 on v2

v3 whole, which is shorter than its diff:
```python
import functools
import math

import jax
import jax.numpy as jnp
from jax import lax
from jax.experimental import pallas as pl
from jax.experimental.pallas import tpu as pltpu
from jax.sharding import PartitionSpec as P

LAGS = 128
HALF = LAGS // 2
EPS = 1e-06
STEP = 16
WHITEN_VMEM = 60 << 20


def whiten_kernel(pairs_hbm, slot_hbm, offset_hbm, raw_hbm, *refs, scale):
    *outs, factor_ref, raw_ref, full, lead, pairs_ref, slot_ref, offset_ref, small, large = refs
    slots, rows, rec = raw_ref.shape
    seg = rec - LAGS
    samples = seg - LAGS
    tiles = pairs_ref.shape[0]
    chunk = 8
    scalars = [
        pltpu.make_async_copy(src, dst, small.at[i])
        for i, (src, dst) in enumerate(
            ((offset_hbm, offset_ref), (pairs_hbm, pairs_ref), (slot_hbm, slot_ref))
        )
    ]
    pieces = [
        pltpu.make_async_copy(
            raw_hbm.at[0, pl.ds(lo, chunk)], raw_ref.at[pl.ds(lo, chunk)], large.at[lo // chunk]
        )
        for lo in range(0, slots, chunk)
    ]
    for one in scalars + pieces:
        one.start()
    owner = lax.axis_index("pairs")
    band = (
        jnp.abs(
            lax.broadcasted_iota(jnp.int32, (seg, seg), 0)
            - lax.broadcasted_iota(jnp.int32, (seg, seg), 1)
        )
        <= HALF
    ).astype(jnp.bfloat16)
    position = lax.broadcasted_iota(jnp.int32, (1, seg), 1)
    tally = jnp.minimum(position, HALF) + jnp.minimum(seg - 1 - position, HALF) + 1
    inverse = 1.0 / tally.astype(jnp.float32)
    scalars[0].wait()
    turn = lax.rem(rec - offset_ref[0], rec)
    for i, piece in enumerate(pieces):
        piece.wait()
        at = slice(i * chunk, (i + 1) * chunk)
        raw = raw_ref[at].reshape(chunk * rows, rec)
        signal = pltpu.roll(raw.astype(jnp.float32), turn, 1)[:, :seg]
        running = jnp.dot(
            jnp.abs(signal).astype(jnp.bfloat16), band, preferred_element_type=jnp.float32
        )
        whitened = signal / (running * inverse + EPS)
        full[at] = whitened.astype(jnp.bfloat16).reshape(chunk, rows, seg)
        lead[at] = (
            whitened[:, HALF : HALF + samples].astype(jnp.bfloat16).reshape(chunk, rows, samples)
        )
    scalars[1].wait()
    scalars[2].wait()
    for t in range(tiles):
        used = jnp.where(pairs_ref[t, 0, owner] >= 0, scale, 0.0)
        factor_ref[t] = jnp.full(factor_ref.shape[1:], used, jnp.float32)
    for k, out in enumerate(outs):
        for t in range(tiles):
            first = slot_ref[jnp.maximum(pairs_ref[t, 0, owner ^ k], 0)]
            second = slot_ref[jnp.maximum(pairs_ref[t, 1, owner ^ k], 0)]
            out[t, :, :seg] = full[second]
            out[t, :, seg:] = lead[first]


def whiten_and_pack(raw_traces, pairs_last, block_slot, win_offset, scale):
    _, slots, rows, rec = raw_traces.shape
    tiles, _, owners = pairs_last.shape
    seg = rec - LAGS
    samples = seg - LAGS
    vmem = pl.BlockSpec(memory_space=pltpu.VMEM)
    return pl.pallas_call(
        functools.partial(whiten_kernel, scale=scale),
        in_specs=[pl.BlockSpec(memory_space=pl.ANY)] * 4,
        out_specs=[vmem] * (owners + 1),
        out_shape=[jax.ShapeDtypeStruct((tiles, rows, seg + samples), jnp.bfloat16)] * owners
        + [jax.ShapeDtypeStruct((tiles, 8, LAGS), jnp.float32)],
        scratch_shapes=[
            pltpu.VMEM((slots, rows, rec), jnp.bfloat16),
            pltpu.VMEM((slots, rows, seg), jnp.bfloat16),
            pltpu.VMEM((slots, rows, samples), jnp.bfloat16),
            pltpu.SMEM(pairs_last.shape, jnp.int32),
            pltpu.SMEM(block_slot.shape, jnp.int32),
            pltpu.SMEM(win_offset.shape, jnp.int32),
            pltpu.SemaphoreType.DMA((3,)),
            pltpu.SemaphoreType.DMA((slots // 8,)),
        ],
        compiler_params=pltpu.CompilerParams(vmem_limit_bytes=WHITEN_VMEM),
        name="whiten",
    )(pairs_last, block_slot, win_offset, raw_traces)


def unit(far, near, owner, t, j, lanes):
    half, _, n, _ = near.shape
    k = owner ^ j
    here = (k < half).astype(jnp.int32) * jnp.ones((n, 1), jnp.int32) > 0
    at = k & (half - 1)
    return jnp.where(here, near[at, t, :, lanes], far[at, t, :, lanes])


def second_block(far, near, owner, t, lanes):
    return jnp.concatenate(
        [unit(far, near, owner, t, j, lanes) for j in range(2 * near.shape[0])], 0
    )


def first_rows(far, near, owner, share, t, rows, lanes):
    n = near.shape[2]
    return jnp.concatenate(
        [unit(far, near, owner, t, share * (rows // n) + j, lanes) for j in range(rows // n)], 0
    )


def turned(row):
    return pltpu.roll(jnp.broadcast_to(row, (STEP, LAGS)), 0, 1, stride=1, stride_axis=0)


def spread(c, lead, toeplitz, windows, samples):
    lane = lax.broadcasted_iota(jnp.int32, (STEP, LAGS), 1)
    early = lane < lax.broadcasted_iota(jnp.int32, (STEP, LAGS), 0)
    at = pl.ds(pl.multiple_of(c * STEP, STEP), STEP)
    for w in range(windows):
        before = 0.0
        row = lead[w, pl.ds(c, 1), :]
        for lo in range(0, samples, LAGS):
            now = turned(row[:, lo : lo + LAGS])
            toeplitz[at, w * samples + lo : w * samples + lo + LAGS] = jnp.where(
                early, before, now
            ).astype(jnp.bfloat16)
            before = now


def held_kernel(*refs, windows):
    far, near = refs[:windows], refs[windows : 2 * windows]
    out_ref, lead, *pairs_of = refs[2 * windows :]
    toeplitz, lagged = pairs_of[:2], pairs_of[2:]
    tiles, blocks, _, chans = out_ref.shape
    _, rows, samples = lead.shape
    seg = samples + LAGS
    rounds = blocks // 2
    per = rows // rounds
    owner, share = lax.axis_index("pairs"), lax.axis_index("win")
    for t in range(-1, tiles):
        if t + 1 < tiles:
            for w in range(windows):
                block = second_block(far[w], near[w], owner, t + 1, slice(0, seg))
                lagged[(t + 1) % 2][w] = block.T
                mine = first_rows(far[w], near[w], owner, share, t + 1, rows, slice(seg, None))
                lead[w] = mine.astype(jnp.float32)

        def step(q, _):
            if t >= 0:
                halves = []
                for b in range(2):
                    lo = pl.multiple_of((2 * q + b) * STEP, STEP)
                    parts = [lagged[t % 2][w, pl.ds(lo, samples), :] for w in range(windows)]
                    halves.append(jnp.concatenate(parts, 0))
                r = jnp.dot(
                    toeplitz[t % 2][...],
                    jnp.concatenate(halves, 1),
                    preferred_element_type=jnp.float32,
                )
                out_ref[t, 2 * q] = r[:, :chans]
                out_ref[t, 2 * q + 1] = r[:, chans:]
            if t + 1 < tiles:
                for i in range(per):
                    spread(q * per + i, lead, toeplitz[(t + 1) % 2], windows, samples)
            return 0

        lax.fori_loop(0, rounds, step, 0, unroll=True)


def stack_kernel(factor_hbm, *refs, windows):
    ins, sums, out_ref = refs[: 2 * windows], refs[2 * windows], refs[2 * windows + 1]
    far, near = ins[:windows], ins[windows:]
    lead, ends, *pairs_of, factor_ref, done, ready = refs[2 * windows + 2 :]
    toeplitz, lagged, lasting, product, staged = (pairs_of[i : i + 2] for i in range(0, 10, 2))
    rows, tiles, chans, _ = out_ref.shape
    new, _, samples = lead.shape
    seg = samples + LAGS
    wide = new * samples
    blocks = LAGS // STEP
    rounds = blocks // 2
    per = rows // rounds
    owner, share = lax.axis_index("pairs"), lax.axis_index("win")
    lane = lax.broadcasted_iota(jnp.int32, (STEP, LAGS), 1)
    shift = lax.broadcasted_iota(jnp.int32, (STEP, LAGS), 0)
    tail = (lax.rem(lane, STEP) < shift) & (lane < windows * STEP)
    factors = pltpu.make_async_copy(factor_hbm, factor_ref, ready.at[0])
    factors.start()

    def prepare(t, s):
        lanes = lax.broadcasted_iota(jnp.int32, (rows, LAGS), 1)
        last = jnp.zeros((rows, LAGS), jnp.float32)
        for w in range(windows):
            fresh = w - (windows - new)
            if fresh >= 0:
                lagged[s][fresh] = second_block(far[w], near[w], owner, t, slice(0, samples)).T
                mine = first_rows(
                    far[w], near[w], owner, share, t, rows, slice(seg, seg + samples)
                ).astype(jnp.float32)
                lead[fresh] = mine
                mine = mine[:, samples - LAGS :]
            else:
                mine = first_rows(
                    far[w], near[w], owner, share, t, rows, slice(2 * samples, None)
                ).astype(jnp.float32)
            lasting[s][w] = second_block(far[w], near[w], owner, t, slice(samples, seg)).T
            at = (w - 1) * STEP % LAGS
            last += jnp.where(
                (lanes >= at) & (lanes < at + STEP),
                pltpu.roll(mine, w * STEP, 1) if w else mine,
                0.0,
            )
        ends[...] = last

    def multiply(q, t, s):
        halves = []
        for b in range(2):
            lo = (2 * q + b) * STEP
            parts = []
            for w in range(new):
                parts += [lagged[s][w, lo:, :], lasting[s][windows - new + w, :lo, :]]
            parts += [lasting[s][w, lo : lo + STEP, :] for w in range(windows)]
            parts.append(jnp.zeros((LAGS - windows * STEP, chans), jnp.bfloat16))
            halves.append(jnp.concatenate([p for p in parts if p.shape[0]], 0))
        r = jnp.dot(
            toeplitz[s][...], jnp.concatenate(halves, 1), preferred_element_type=jnp.float32
        )
        product[s][2 * q] = r[:, :chans] + sums[t, 2 * q]
        product[s][2 * q + 1] = r[:, chans:] + sums[t, 2 * q + 1]

    def finish(c, s, factor):
        at = pl.ds(c * STEP, STEP)
        staged[s][c] = product[s][:, at, :].reshape(LAGS, chans).T * factor

    def copy(t):
        return pltpu.make_async_copy(staged[t % 2], out_ref.at[:, t], done.at[t % 2])

    for t in range(-1, tiles + 1):
        if t + 1 < tiles:
            prepare(t + 1, (t + 1) % 2)
        if t == 1:
            factors.wait()
        if t >= 1:
            factor = factor_ref[t - 1, 0:1, :]
            if t >= 3:
                copy(t - 3).wait()
        for q in range(rounds):
            if 0 <= t < tiles:
                multiply(q, t, t % 2)
            for c in range(q * per, (q + 1) * per):
                if t + 1 < tiles:
                    spread(c, lead, toeplitz[(t + 1) % 2], new, samples)
                    toeplitz[(t + 1) % 2][c * STEP : (c + 1) * STEP, wide:] = jnp.where(
                        tail, turned(ends[c : c + 1, :]), 0.0
                    ).astype(jnp.bfloat16)
                if t >= 1:
                    finish(c, (t - 1) % 2, factor)
        if t >= 1:
            copy(t - 1).start()
    for t in range(max(tiles - 2, 0), tiles):
        copy(t).wait()


def stack(factor, held, brought, rows, chans):
    _, tiles, n, width = held[0][0].shape
    samples = (width - LAGS) // 2
    seg = samples + LAGS
    depth = rows * STEP
    windows, old, new = len(held) + len(brought), len(held), len(brought)
    vmem = pl.BlockSpec(memory_space=pltpu.VMEM)
    hbm = pl.BlockSpec(memory_space=pl.ANY)

    def flat(groups):
        return [g[0] for g in groups] + [g[1] for g in groups]

    flops = 2 * tiles * depth * samples * chans * (LAGS // STEP)
    sums = pl.pallas_call(
        functools.partial(held_kernel, windows=old),
        in_specs=[vmem] * (2 * old),
        out_specs=vmem,
        out_shape=jax.ShapeDtypeStruct((tiles, LAGS // STEP, depth, chans), jnp.float32),
        scratch_shapes=[pltpu.VMEM((old, rows, samples), jnp.float32)]
        + [pltpu.VMEM((depth, old * samples), jnp.bfloat16)] * 2
        + [pltpu.VMEM((old, seg, chans), jnp.bfloat16)] * 2,
        compiler_params=pltpu.CompilerParams(vmem_limit_bytes=24 << 20),
        cost_estimate=pl.CostEstimate(
            flops=old * flops, bytes_accessed=8 << 20, transcendentals=0
        ),
        name="held",
    )(*flat(held))
    return pl.pallas_call(
        functools.partial(stack_kernel, windows=windows),
        in_specs=[hbm] + [vmem] * (2 * windows + 1),
        out_specs=hbm,
        out_shape=jax.ShapeDtypeStruct((rows, tiles, chans, LAGS), jnp.float32),
        scratch_shapes=[
            pltpu.VMEM((new, rows, samples), jnp.float32),
            pltpu.VMEM((rows, LAGS), jnp.float32),
        ]
        + [pltpu.VMEM((depth, new * samples + LAGS), jnp.bfloat16)] * 2
        + [pltpu.VMEM((new, samples, chans), jnp.bfloat16)] * 2
        + [pltpu.VMEM((windows, LAGS, chans), jnp.bfloat16)] * 2
        + [pltpu.VMEM((LAGS // STEP, depth, chans), jnp.float32)] * 2
        + [pltpu.VMEM((rows, chans, LAGS), jnp.float32)] * 2
        + [
            pltpu.VMEM(factor.shape, jnp.float32),
            pltpu.SemaphoreType.DMA((2,)),
            pltpu.SemaphoreType.DMA((1,)),
        ],
        compiler_params=pltpu.CompilerParams(vmem_limit_bytes=24 << 20),
        name="stack",
    )(factor, *flat(held + brought), sums)


def body(raw_traces, tile_pairs, block_slot, win_offset):
    owners = lax.axis_size("pairs")
    windows = lax.axis_size("win")
    rows, rec = raw_traces.shape[2:]
    chans = rows * owners
    samples = rec - 2 * LAGS
    pairs_last = jnp.transpose(tile_pairs, (1, 2, 0))
    scale = 1.0 / math.sqrt(windows * samples)
    *units, factor = whiten_and_pack(raw_traces, pairs_last, block_slot, win_offset, scale)

    def swap(x, axis, size, k):
        return lax.ppermute(x, axis, [(i, i ^ k) for i in range(size)])

    units = [u if k == 0 else swap(u, "pairs", owners, k) for k, u in enumerate(units)]
    held, brought = [], []
    for low in (owners // 2, 0):
        own = jnp.stack(units[low : low + owners // 2])
        other = swap(own, "win", windows, 2)
        held.append((own, swap(own, "win", windows, 1)))
        brought.append((other, swap(other, "win", windows, 1)))
    return stack(factor, list(zip(*held)), list(zip(*brought)), chans // windows, chans)


def plain_whiten(signal):
    length = signal.shape[-1]
    seg_count = length // LAGS
    magnitude = jnp.abs(signal).reshape(signal.shape[:-1] + (seg_count, LAGS))
    padded = jnp.pad(magnitude, [(0, 0)] * (magnitude.ndim - 2) + [(1, 1), (0, 0)])
    windows = jnp.concatenate([padded[..., :-2, :], padded[..., 1:-1, :], padded[..., 2:, :]], -1)
    rowpos = jnp.arange(3 * LAGS)[:, None]
    colpos = jnp.arange(LAGS)[None, :]
    band_matrix = (jnp.abs(rowpos - LAGS - colpos) <= HALF).astype(jnp.float32)
    totals = jnp.einsum(
        "...ni,ij->...nj", windows, band_matrix, precision=lax.Precision.HIGHEST
    ).reshape(signal.shape)
    position = jnp.arange(length)
    tally = (jnp.minimum(position, HALF) + jnp.minimum(length - 1 - position, HALF) + 1).astype(
        jnp.float32
    )
    return (signal / (totals / tally + EPS)).astype(jnp.bfloat16)


def plain_correlate(leading_blocks, trailing_blocks):
    seg_len = leading_blocks.shape[-1]
    samples = seg_len - LAGS
    kernel = jnp.transpose(leading_blocks[..., HALF : HALF + samples], (1, 0, 2))
    source = jnp.transpose(trailing_blocks[..., : seg_len - 1], (1, 0, 2))
    return lax.conv_general_dilated(
        source,
        kernel,
        (1,),
        "VALID",
        dimension_numbers=("NCH", "OIH", "CNH"),
        preferred_element_type=jnp.float32,
    )


def plain_body(raw_traces, tile_pairs, block_slot, win_offset):
    owner_index = lax.axis_index("pairs")
    pair_count = lax.axis_size("pairs")
    win_count = lax.axis_size("win")
    local_channels = raw_traces.shape[2]
    channels = local_channels * pair_count
    seg_len = raw_traces.shape[3] - LAGS
    samples = seg_len - LAGS
    tile_count = tile_pairs.shape[1]
    segment = lax.dynamic_slice_in_dim(raw_traces[0], win_offset[0], seg_len, 2).astype(jnp.float32)
    whitened = plain_whiten(segment)
    wanted = tile_pairs.reshape(pair_count, 2 * tile_count)
    slot_index = block_slot[jnp.maximum(wanted, 0)]
    outgoing = jnp.take(whitened, slot_index.reshape(-1), axis=0).reshape(
        pair_count, 2 * tile_count, local_channels, seg_len
    )
    incoming = lax.all_to_all(outgoing, "pairs", split_axis=0, concat_axis=2, tiled=True)
    blocks = incoming[0].reshape(tile_count, 2, channels, seg_len)
    own_tiles = lax.dynamic_index_in_dim(tile_pairs, owner_index, 0, keepdims=False)
    tile_valid = (own_tiles[:, 0] >= 0).astype(jnp.float32)
    firsts = blocks[:, 0]
    seconds = blocks[:, 1]
    spread_rows = lax.all_to_all(firsts[:, None], "win", split_axis=2, concat_axis=1, tiled=True)
    piece = lax.all_gather(seconds[:, None], "win", axis=1, tiled=True)
    summed = jnp.stack(
        [plain_correlate(spread_rows[tile], piece[tile]) for tile in range(tile_count)], 1
    )
    scale = 1.0 / math.sqrt(win_count * samples)
    return summed * scale * tile_valid[None, :, None, None]


def solution(mesh):
    regular = mesh.shape["pairs"] == 8 and mesh.shape["win"] == 4
    return jax.shard_map(
        body if regular else plain_body,
        mesh=mesh,
        in_specs=(P("win", None, "pairs", None), P(), P(), P("win")),
        out_specs=P("win", "pairs", None, None),
        check_vma=False,
    )
```

time: 48.2 us -> 45.9 us (0.952)
  local copies, waits for them, and re-layouts: 2.53 us -> 0.01 us
  waiting for transfers between devices: 19.2 us -> 17.3 us
  Pallas kernels: 12.2 us -> 13.5 us
  other arithmetic: 0.18 us -> 0.99 us
    unnamed x5 -> x2, local copies, waits for them, and re-layouts: 2.53 us -> 0.01 us
    ppermute x13, waiting for transfers between devices: 19.2 us -> 17.3 us  [swap(): return lax.ppermute(x, axis, [(i, i ^ k) for i in range(size)])]
    pallas_call x2 -> x3, Pallas kernels: 12.2 us -> 13.5 us  [the longest x1 7.21 us: stack(): pl.pallas_call(functools.partial(stack_kernel, windows=windows), in_specs...]
    another operation x3 -> x2, other arithmetic: 0.18 us -> 0.99 us  [body(): own = jnp.stack(units[low:low + owners // 2])]
  transfers between devices with their start and end apart: 13 -> 13, of which waited for: 5 -> 3; matrix products, arithmetic and copies ran while one was open for 0% -> 2% of each run, Pallas kernels for 0% -> 5%
where the time goes in v3:
time: 45.9 us; the launch traced here: 45.7 us
  waiting for transfers between devices  17.3 us (38%)
  Pallas kernels  13.5 us (29%)
  starting transfers between devices  13.2 us (29%)
  other arithmetic  0.99 us (2%)
  between operations  0.72 us (2%)
    ppermute x13, waiting for transfers between devices, swap(): return lax.ppermute(x, axis, [(i, i ^ k) for i in range(size)])  17.3 us
    ppermute x13, starting transfers between devices, swap(): return lax.ppermute(x, axis, [(i, i ^ k) for i in range(size)])  13.2 us
    pallas_call x1, Pallas kernels, stack(): pl.pallas_call(functools.partial(stack_kernel, windows=windows), in_specs...  7.21 us
    pallas_call x1, Pallas kernels, whiten_and_pack(): pl.pallas_call(functools.partial(whiten_kernel, scale=scale), in_specs=[p...  3.86 us
    pallas_call x1, Pallas kernels, stack(): pl.pallas_call(functools.partial(held_kernel, windows=old), in_specs=[vme...  2.47 us
    another operation x2, other arithmetic, body(): own = jnp.stack(units[low:low + owners // 2])  0.99 us
  transfers between devices with their start and end apart: 13, of which 3 were waited for; matrix products, arithmetic and copies ran while one was open for 2% of the time, Pallas kernels for 5%

profile of v3, /device:TPU:17, one launch (start us, length us, event | category | flops | bytes accessed | tf_op | source)
XLA Modules:
  0.0 45.7 jit_solution(14056488975056906667)
XLA Ops:
  0.7 3.9 %whiten.1 = (bf16[4,16,640]{2,1,0:T(8,128)(2,1)}, bf16[4,16,640]{2,1,0:T(8,128)(2,1)}, bf16[4,16,640]{2,1,0:T(8,128)(2,1)}, bf16[4,16,640]{2,1,0:T(8,128)(2,1)},...) custom-call(s32[4,2,8]{2,1,0:T(2,128)} %bitcast.17, ...), custom_call_target="tpu_custom_call" | custom-call | tf_op jit(solution)/shard_map/whiten/pallas_call | solution.py:84
  4.5 0.0 copy-start
  4.5 1.3 %collective-permute-start.7 = (bf16[4,16,640]{2,1,0:T(8,128)(2,1)}, bf16[4,16,640]{2,1,0:T(8,128)(2,1)S(1)}, u32[]{:S(2)}, u32[]{:S(2)}) collective-permute-start(bf16[4,16,640]{2,1,0:T(8,128)(2,1)} %get-tuple-element.20), channel_id=1, source_target_pairs={{0,4},{4,0},{8,12},{12,8},{16,20},{20,16},{24,28},{28,24},{1,5},{5... | collective-permute-start | bytes 245768 | tf_op jit(solution)/shard_map/ppermute | solution.py:340
  5.8 1.3 %collective-permute-start.8 = (bf16[4,16,640]{2,1,0:T(8,128)(2,1)}, bf16[4,16,640]{2,1,0:T(8,128)(2,1)S(1)}, u32[]{:S(2)}, u32[]{:S(2)}) collective-permute-start(bf16[4,16,640]{2,1,0:T(8,128)(2,1)} %get-tuple-element.21), channel_id=1, source_target_pairs={{0,8},{4,12},{8,0},{12,4},{16,24},{20,28},{24,16},{28,20},{1,9},{5... | collective-permute-start | bytes 245768 | tf_op jit(solution)/shard_map/ppermute | solution.py:340
  7.1 0.1 collective-permute-start.9
  7.2 0.0 collective-permute-start
  7.2 3.3 %collective-permute-start.1 = (bf16[4,16,640]{2,1,0:T(8,128)(2,1)}, bf16[4,16,640]{2,1,0:T(8,128)(2,1)S(1)}, u32[]{:S(2)}, u32[]{:S(2)}) collective-permute-start(bf16[4,16,640]{2,1,0:T(8,128)(2,1)} %get-tuple-element.16), channel_id=1, source_target_pairs={{0,20},{4,16},{8,28},{12,24},{16,4},{20,0},{24,12},{28,8},{1,21},{... | collective-permute-start | bytes 245768 | tf_op jit(solution)/shard_map/ppermute | solution.py:340
  10.5 0.0 collective-permute-done.7
  10.5 0.2 collective-permute-start.2
  10.7 0.0 collective-permute-done.8
  10.7 1.3 %collective-permute-start.3 = (bf16[4,16,640]{2,1,0:T(8,128)(2,1)}, bf16[4,16,640]{2,1,0:T(8,128)(2,1)S(1)}, u32[]{:S(2)}, u32[]{:S(2)}) collective-permute-start(bf16[4,16,640]{2,1,0:T(8,128)(2,1)} %get-tuple-element.18), channel_id=1, source_target_pairs={{0,28},{4,24},{8,20},{12,16},{16,12},{20,8},{24,4},{28,0},{1,29},{... | collective-permute-start | bytes 245768 | tf_op jit(solution)/shard_map/ppermute | solution.py:340
  12.0 0.0 collective-permute-done.9
  12.0 0.9 %pad_maximum_fusion.1.refs_2_.refs_4_ = bf16[4,4,16,640]{3,2,1,0:T(8,128)(2,1)S(1)} fusion(bf16[1,4,16,640]{3,2,1,0:T(8,128)(2,1)S(1)} %bitcast.16, bf16[1,4,16,640]{3,2,1,0:T(8,128)(2,1)S(1)} %bitcast.14, bf16[1,4,16,640]{3,2,1,0:T(8,128)(2,1)S(1)} %bitcast.13, bf16[1,4,16,640]{3,2,1,0:T(8,128)(2,1)} %bitcast.10), kind=kLoop, calls=%fused_computation.1 | loop fusion | flops 491520 | bytes 655360 | tf_op jit(solution)/shard_map/stack | solution.py:345
  12.9 1.3 %collective-permute-start.11 = (bf16[4,4,16,640]{3,2,1,0:T(8,128)(2,1)S(1)}, bf16[4,4,16,640]{3,2,1,0:T(8,128)(2,1)S(1)}, u32[]{:S(2)}, u32[]{:S(2)}) collective-permute-start(bf16[4,4,16,640]{3,2,1,0:T(8,128)(2,1)S(1)} %pad_maximum_fusion.1.refs_2_.refs_4_), channel_id=1, source_target_pairs={{0,2},{1,3},{2,0},{3,1},{4,6},{5,7},{6,4},{7,5},{8,10},{9,11},{10,... | collective-permute-start | bytes 983048 | tf_op jit(solution)/shard_map/ppermute | solution.py:340
  14.2 0.0 collective-permute-done
  14.2 0.0 collective-permute-done.1
  14.2 8.1 %collective-permute-done.2 = bf16[4,16,640]{2,1,0:T(8,128)(2,1)S(1)} collective-permute-done((bf16[4,16,640]{2,1,0:T(8,128)(2,1)}, bf16[4,16,640]{2,1,0:T(8,128)(2,1)S(1)}, u32[]{:S(2)}, u32[]{:S(2)}) %collective-permute-start.2) | collective-permute-done | bytes 81952 | tf_op jit(solution)/shard_map/ppermute | solution.py:340
  22.3 3.4 %collective-permute-done.3 = bf16[4,16,640]{2,1,0:T(8,128)(2,1)S(1)} collective-permute-done((bf16[4,16,640]{2,1,0:T(8,128)(2,1)}, bf16[4,16,640]{2,1,0:T(8,128)(2,1)S(1)}, u32[]{:S(2)}, u32[]{:S(2)}) %collective-permute-start.3) | collective-permute-done | bytes 81952 | tf_op jit(solution)/shard_map/ppermute | solution.py:340
  25.8 0.1 pad_maximum_fusion.refs_0_
  25.8 1.3 %collective-permute-start.5 = (bf16[4,4,16,640]{3,2,1,0:T(8,128)(2,1)S(1)}, bf16[4,4,16,640]{3,2,1,0:T(8,128)(2,1)S(1)}, u32[]{:S(2)}, u32[]{:S(2)}) collective-permute-start(bf16[4,4,16,640]{3,2,1,0:T(8,128)(2,1)S(1)} %pad_maximum_fusion.refs_0_), channel_id=1, source_target_pairs={{0,2},{1,3},{2,0},{3,1},{4,6},{5,7},{6,4},{7,5},{8,10},{9,11},{10,... | collective-permute-start | bytes 983048 | tf_op jit(solution)/shard_map/ppermute | solution.py:340
  27.1 1.0 %collective-permute-start.10 = (bf16[4,4,16,640]{3,2,1,0:T(8,128)(2,1)S(1)}, bf16[4,4,16,640]{3,2,1,0:T(8,128)(2,1)S(1)}, u32[]{:S(2)}, u32[]{:S(2)}) collective-permute-start(bf16[4,4,16,640]{3,2,1,0:T(8,128)(2,1)S(1)} %pad_maximum_fusion.1.refs_2_.refs_4_), channel_id=1, source_target_pairs={{0,1},{1,0},{2,3},{3,2},{4,5},{5,4},{6,7},{7,6},{8,9},{9,8},{10,11... | collective-permute-start | bytes 983048 | tf_op jit(solution)/shard_map/ppermute | solution.py:340
  28.2 0.0 collective-permute-start.4
  28.2 0.0 collective-permute-done.11.refs_6_
  28.2 0.5 %collective-permute-start.12 = (bf16[4,4,16,640]{3,2,1,0:T(8,128)(2,1)S(1)}, bf16[4,4,16,640]{3,2,1,0:T(8,128)(2,1)S(1)}, u32[]{:S(2)}, u32[]{:S(2)}) collective-permute-start(bf16[4,4,16,640]{3,2,1,0:T(8,128)(2,1)S(1)} %collective-permute-done.11.refs_6_), channel_id=1, source_target_pairs={{0,1},{1,0},{2,3},{3,2},{4,5},{5,4},{6,7},{7,6},{8,9},{9,8},{10,11... | collective-permute-start | bytes 983048 | tf_op jit(solution)/shard_map/ppermute | solution.py:340
  28.7 5.7 %collective-permute-done.5.refs_2_ = bf16[4,4,16,640]{3,2,1,0:T(8,128)(2,1)S(1)} collective-permute-done((bf16[4,4,16,640]{3,2,1,0:T(8,128)(2,1)S(1)}, bf16[4,4,16,640]{3,2,1,0:T(8,128)(2,1)S(1)}, u32[]{:S(2)}, u32[]{:S(2)}) %collective-permute-start.5) | collective-permute-done | bytes 327712 | tf_op jit(solution)/shard_map/ppermute | solution.py:340
  34.4 1.6 %collective-permute-start.6 = (bf16[4,4,16,640]{3,2,1,0:T(8,128)(2,1)S(1)}, bf16[4,4,16,640]{3,2,1,0:T(8,128)(2,1)S(1)}, u32[]{:S(2)}, u32[]{:S(2)}) collective-permute-start(bf16[4,4,16,640]{3,2,1,0:T(8,128)(2,1)S(1)} %collective-permute-done.5.refs_2_), channel_id=1, source_target_pairs={{0,1},{1,0},{2,3},{3,2},{4,5},{5,4},{6,7},{7,6},{8,9},{9,8},{10,11... | collective-permute-start | bytes 983048 | tf_op jit(solution)/shard_map/ppermute | solution.py:340
  36.0 0.0 collective-permute-done.10.refs_3_.refs_5_
  36.0 0.0 collective-permute-done.4.refs_1_
  36.0 2.5 %held.1.refs_8_ = f32[4,8,512,128]{3,2,1,0:T(8,128)S(1)} custom-call(bf16[4,4,16,640]{3,2,1,0:T(8,128)(2,1)S(1)} %pad_maximum_fusion.refs_0_, bf16[4,4,16,640]{3,2,1,0:T(8,128)(2,1)S(1)} %collective-permute-done.4.refs_1_, bf16[4,4,16,640]{3,2,1,0:T(8,128)(2,1)S(1)} %pad_maximum_fusion.1.refs_2_.refs_4_, ...), custom_call_target="tpu_custom_call" | custom-call | flops 2147483648 | bytes 8388608 | tf_op jit(solution)/shard_map/held/pallas_call | solution.py:291
  38.5 0.0 collective-permute-done.12.refs_7_
  38.5 0.0 collective-permute-done.6.refs_3_
  38.5 7.2 %stack.41 = f32[32,4,128,128]{3,2,1,0:T(8,128)} custom-call(f32[4,8,128]{2,1,0:T(8,128)S(1)} %copy-done, bf16[4,4,16,640]{3,2,1,0:T(8,128)(2,1)S(1)} %pad_maximum_fusion.refs_0_, bf16[4,4,16,640]{3,2,1,0:T(8,128)(2,1)S(1)} %collective-permute-done.4.refs_1_, bf16[4,4,16,640]{3,2,1,0:T(8,128)(2,1)S(1)} %collective-permute-done.5.refs_2_, ...), custom_call_target="tpu_custom_call" | custom-call | tf_op jit(solution)/shard_map/stack/pallas_call | solution.py:305
  (1 shorter events, 0.0 us)
Async XLA Ops:
  4.5 34.0 %copy-start = (f32[4,8,128]{2,1,0:T(8,128)S(1)}, f32[4,8,128]{2,1,0:T(8,128)}, u32[]{:S(2)}) copy-start(f32[4,8,128]{2,1,0:T(8,128)} %get-tuple-element.14.factor_hbm) | copy-start | bytes 49156
  4.5 6.0 %collective-permute-start.7 = (bf16[4,16,640]{2,1,0:T(8,128)(2,1)}, bf16[4,16,640]{2,1,0:T(8,128)(2,1)S(1)}, u32[]{:S(2)}, u32[]{:S(2)}) collective-permute-start(bf16[4,16,640]{2,1,0:T(8,128)(2,1)} %get-tuple-element.20), channel_id=1, source_target_pairs={{0,4},{4,0},{8,12},{12,8},{16,20},{20,16},{24,28},{28,24},{1,5},{5... | collective-permute-start | bytes 245768 | tf_op jit(solution)/shard_map/ppermute | solution.py:340
  5.8 4.9 %collective-permute-start.8 = (bf16[4,16,640]{2,1,0:T(8,128)(2,1)}, bf16[4,16,640]{2,1,0:T(8,128)(2,1)S(1)}, u32[]{:S(2)}, u32[]{:S(2)}) collective-permute-start(bf16[4,16,640]{2,1,0:T(8,128)(2,1)} %get-tuple-element.21), channel_id=1, source_target_pairs={{0,8},{4,12},{8,0},{12,4},{16,24},{20,28},{24,16},{28,20},{1,9},{5... | collective-permute-start | bytes 245768 | tf_op jit(solution)/shard_map/ppermute | solution.py:340
  7.1 4.9 %collective-permute-start.9 = (bf16[4,16,640]{2,1,0:T(8,128)(2,1)}, bf16[4,16,640]{2,1,0:T(8,128)(2,1)S(1)}, u32[]{:S(2)}, u32[]{:S(2)}) collective-permute-start(bf16[4,16,640]{2,1,0:T(8,128)(2,1)} %get-tuple-element.22), channel_id=1, source_target_pairs={{0,12},{4,8},{8,4},{12,0},{16,28},{20,24},{24,20},{28,16},{1,13},{... | collective-permute-start | bytes 245768 | tf_op jit(solution)/shard_map/ppermute | solution.py:340
  7.2 7.0 %collective-permute-start = (bf16[4,16,640]{2,1,0:T(8,128)(2,1)}, bf16[4,16,640]{2,1,0:T(8,128)(2,1)S(1)}, u32[]{:S(2)}, u32[]{:S(2)}) collective-permute-start(bf16[4,16,640]{2,1,0:T(8,128)(2,1)} %get-tuple-element.15), channel_id=1, source_target_pairs={{0,16},{4,20},{8,24},{12,28},{16,0},{20,4},{24,8},{28,12},{1,17},{... | collective-permute-start | bytes 245768 | tf_op jit(solution)/shard_map/ppermute | solution.py:340
  7.2 7.0 %collective-permute-start.1 = (bf16[4,16,640]{2,1,0:T(8,128)(2,1)}, bf16[4,16,640]{2,1,0:T(8,128)(2,1)S(1)}, u32[]{:S(2)}, u32[]{:S(2)}) collective-permute-start(bf16[4,16,640]{2,1,0:T(8,128)(2,1)} %get-tuple-element.16), channel_id=1, source_target_pairs={{0,20},{4,16},{8,28},{12,24},{16,4},{20,0},{24,12},{28,8},{1,21},{... | collective-permute-start | bytes 245768 | tf_op jit(solution)/shard_map/ppermute | solution.py:340
  10.5 11.8 %collective-permute-start.2 = (bf16[4,16,640]{2,1,0:T(8,128)(2,1)}, bf16[4,16,640]{2,1,0:T(8,128)(2,1)S(1)}, u32[]{:S(2)}, u32[]{:S(2)}) collective-permute-start(bf16[4,16,640]{2,1,0:T(8,128)(2,1)} %get-tuple-element.17), channel_id=1, source_target_pairs={{0,24},{4,28},{8,16},{12,20},{16,8},{20,12},{24,0},{28,4},{1,25},{... | collective-permute-start | bytes 245768 | tf_op jit(solution)/shard_map/ppermute | solution.py:340
  10.7 15.1 %collective-permute-start.3 = (bf16[4,16,640]{2,1,0:T(8,128)(2,1)}, bf16[4,16,640]{2,1,0:T(8,128)(2,1)S(1)}, u32[]{:S(2)}, u32[]{:S(2)}) collective-permute-start(bf16[4,16,640]{2,1,0:T(8,128)(2,1)} %get-tuple-element.18), channel_id=1, source_target_pairs={{0,28},{4,24},{8,20},{12,16},{16,12},{20,8},{24,4},{28,0},{1,29},{... | collective-permute-start | bytes 245768 | tf_op jit(solution)/shard_map/ppermute | solution.py:340
  12.9 15.2 %collective-permute-start.11 = (bf16[4,4,16,640]{3,2,1,0:T(8,128)(2,1)S(1)}, bf16[4,4,16,640]{3,2,1,0:T(8,128)(2,1)S(1)}, u32[]{:S(2)}, u32[]{:S(2)}) collective-permute-start(bf16[4,4,16,640]{3,2,1,0:T(8,128)(2,1)S(1)} %pad_maximum_fusion.1.refs_2_.refs_4_), channel_id=1, source_target_pairs={{0,2},{1,3},{2,0},{3,1},{4,6},{5,7},{6,4},{7,5},{8,10},{9,11},{10,... | collective-permute-start | bytes 983048 | tf_op jit(solution)/shard_map/ppermute | solution.py:340
  25.8 8.6 %collective-permute-start.5 = (bf16[4,4,16,640]{3,2,1,0:T(8,128)(2,1)S(1)}, bf16[4,4,16,640]{3,2,1,0:T(8,128)(2,1)S(1)}, u32[]{:S(2)}, u32[]{:S(2)}) collective-permute-start(bf16[4,4,16,640]{3,2,1,0:T(8,128)(2,1)S(1)} %pad_maximum_fusion.refs_0_), channel_id=1, source_target_pairs={{0,2},{1,3},{2,0},{3,1},{4,6},{5,7},{6,4},{7,5},{8,10},{9,11},{10,... | collective-permute-start | bytes 983048 | tf_op jit(solution)/shard_map/ppermute | solution.py:340
  27.1 8.9 %collective-permute-start.10 = (bf16[4,4,16,640]{3,2,1,0:T(8,128)(2,1)S(1)}, bf16[4,4,16,640]{3,2,1,0:T(8,128)(2,1)S(1)}, u32[]{:S(2)}, u32[]{:S(2)}) collective-permute-start(bf16[4,4,16,640]{3,2,1,0:T(8,128)(2,1)S(1)} %pad_maximum_fusion.1.refs_2_.refs_4_), channel_id=1, source_target_pairs={{0,1},{1,0},{2,3},{3,2},{4,5},{5,4},{6,7},{7,6},{8,9},{9,8},{10,11... | collective-permute-start | bytes 983048 | tf_op jit(solution)/shard_map/ppermute | solution.py:340
  28.2 7.9 %collective-permute-start.4 = (bf16[4,4,16,640]{3,2,1,0:T(8,128)(2,1)S(1)}, bf16[4,4,16,640]{3,2,1,0:T(8,128)(2,1)S(1)}, u32[]{:S(2)}, u32[]{:S(2)}) collective-permute-start(bf16[4,4,16,640]{3,2,1,0:T(8,128)(2,1)S(1)} %pad_maximum_fusion.refs_0_), channel_id=1, source_target_pairs={{0,1},{1,0},{2,3},{3,2},{4,5},{5,4},{6,7},{7,6},{8,9},{9,8},{10,11... | collective-permute-start | bytes 983048 | tf_op jit(solution)/shard_map/ppermute | solution.py:340
  28.2 10.3 %collective-permute-start.12 = (bf16[4,4,16,640]{3,2,1,0:T(8,128)(2,1)S(1)}, bf16[4,4,16,640]{3,2,1,0:T(8,128)(2,1)S(1)}, u32[]{:S(2)}, u32[]{:S(2)}) collective-permute-start(bf16[4,4,16,640]{3,2,1,0:T(8,128)(2,1)S(1)} %collective-permute-done.11.refs_6_), channel_id=1, source_target_pairs={{0,1},{1,0},{2,3},{3,2},{4,5},{5,4},{6,7},{7,6},{8,9},{9,8},{10,11... | collective-permute-start | bytes 983048 | tf_op jit(solution)/shard_map/ppermute | solution.py:340
  34.4 4.1 %collective-permute-start.6 = (bf16[4,4,16,640]{3,2,1,0:T(8,128)(2,1)S(1)}, bf16[4,4,16,640]{3,2,1,0:T(8,128)(2,1)S(1)}, u32[]{:S(2)}, u32[]{:S(2)}) collective-permute-start(bf16[4,4,16,640]{3,2,1,0:T(8,128)(2,1)S(1)} %collective-permute-done.5.refs_2_), channel_id=1, source_target_pairs={{0,1},{1,0},{2,3},{3,2},{4,5},{5,4},{6,7},{7,6},{8,9},{9,8},{10,11... | collective-permute-start | bytes 983048 | tf_op jit(solution)/shard_map/ppermute | solution.py:340

commit v4 on v3

--- a/solution.py
+++ b/solution.py
@@ -16,25 +16,19 @@
 
 
 def whiten_kernel(pairs_hbm, slot_hbm, offset_hbm, raw_hbm, *refs, scale):
-    *outs, factor_ref, raw_ref, full, lead, pairs_ref, slot_ref, offset_ref, small, large = refs
+    *outs, factor_ref, raw_ref, full, lead, pairs_ref, slot_ref, offset_ref, sems = refs
     slots, rows, rec = raw_ref.shape
     seg = rec - LAGS
     samples = seg - LAGS
     tiles = pairs_ref.shape[0]
-    chunk = 8
     scalars = [
-        pltpu.make_async_copy(src, dst, small.at[i])
+        pltpu.make_async_copy(src, dst, sems.at[i])
         for i, (src, dst) in enumerate(
             ((offset_hbm, offset_ref), (pairs_hbm, pairs_ref), (slot_hbm, slot_ref))
         )
     ]
-    pieces = [
-        pltpu.make_async_copy(
-            raw_hbm.at[0, pl.ds(lo, chunk)], raw_ref.at[pl.ds(lo, chunk)], large.at[lo // chunk]
-        )
-        for lo in range(0, slots, chunk)
-    ]
-    for one in scalars + pieces:
+    record = pltpu.make_async_copy(raw_hbm.at[0], raw_ref, sems.at[3])
+    for one in [record] + scalars:
         one.start()
     owner = lax.axis_index("pairs")
     band = (
@@ -49,19 +43,15 @@
     inverse = 1.0 / tally.astype(jnp.float32)
     scalars[0].wait()
     turn = lax.rem(rec - offset_ref[0], rec)
-    for i, piece in enumerate(pieces):
-        piece.wait()
-        at = slice(i * chunk, (i + 1) * chunk)
-        raw = raw_ref[at].reshape(chunk * rows, rec)
-        signal = pltpu.roll(raw.astype(jnp.float32), turn, 1)[:, :seg]
-        running = jnp.dot(
-            jnp.abs(signal).astype(jnp.bfloat16), band, preferred_element_type=jnp.float32
-        )
-        whitened = signal / (running * inverse + EPS)
-        full[at] = whitened.astype(jnp.bfloat16).reshape(chunk, rows, seg)
-        lead[at] = (
-            whitened[:, HALF : HALF + samples].astype(jnp.bfloat16).reshape(chunk, rows, samples)
-        )
+    record.wait()
+    raw = raw_ref[...].reshape(slots * rows, rec)
+    signal = pltpu.roll(raw.astype(jnp.float32), turn, 1)[:, :seg]
+    running = jnp.dot(
+        jnp.abs(signal).astype(jnp.bfloat16), band, preferred_element_type=jnp.float32
+    )
+    whitened = signal / (running * inverse + EPS)
+    full[...] = whitened.astype(jnp.bfloat16).reshape(slots, rows, seg)
+    lead[...] = whitened[:, HALF : HALF + samples].astype(jnp.bfloat16).reshape(slots, rows, samples)
     scalars[1].wait()
     scalars[2].wait()
     for t in range(tiles):
@@ -94,8 +84,7 @@
             pltpu.SMEM(pairs_last.shape, jnp.int32),
             pltpu.SMEM(block_slot.shape, jnp.int32),
             pltpu.SMEM(win_offset.shape, jnp.int32),
-            pltpu.SemaphoreType.DMA((3,)),
-            pltpu.SemaphoreType.DMA((slots // 8,)),
+            pltpu.SemaphoreType.DMA((4,)),
         ],
         compiler_params=pltpu.CompilerParams(vmem_limit_bytes=WHITEN_VMEM),
         name="whiten",

time: 45.9 us -> 44.9 us (0.978)
  Pallas kernels: 13.5 us -> 12.5 us
    pallas_call x1, Pallas kernels: 3.86 us -> 2.85 us  [whiten_and_pack(): pl.pallas_call(functools.partial(whiten_kernel, scale=scale), in_specs=[p...]
  transfers between devices with their start and end apart: 13 -> 13, of which waited for: 3 -> 3; matrix products, arithmetic and copies ran while one was open for 2% -> 2% of each run, Pallas kernels for 5% -> 6%
where the time goes in v4:
time: 44.9 us; the launch traced here: 44.7 us
  waiting for transfers between devices  17.3 us (39%)
  starting transfers between devices  13.2 us (29%)
  Pallas kernels  12.5 us (28%)
  other arithmetic  0.99 us (2%)
  between operations  0.72 us (2%)
    ppermute x13, waiting for transfers between devices, swap(): return lax.ppermute(x, axis, [(i, i ^ k) for i in range(size)])  17.3 us
    ppermute x13, starting transfers between devices, swap(): return lax.ppermute(x, axis, [(i, i ^ k) for i in range(size)])  13.2 us
    pallas_call x1, Pallas kernels, stack(): pl.pallas_call(functools.partial(stack_kernel, windows=windows), in_specs...  7.2 us
    pallas_call x1, Pallas kernels, whiten_and_pack(): pl.pallas_call(functools.partial(whiten_kernel, scale=scale), in_specs=[p...  2.85 us
    pallas_call x1, Pallas kernels, stack(): pl.pallas_call(functools.partial(held_kernel, windows=old), in_specs=[vme...  2.47 us
    another operation x2, other arithmetic, body(): own = jnp.stack(units[low:low + owners // 2])  0.99 us
  transfers between devices with their start and end apart: 13, of which 3 were waited for; matrix products, arithmetic and copies ran while one was open for 2% of the time, Pallas kernels for 6%

profile of v4, /device:TPU:17, one launch (start us, length us, event | category | flops | bytes accessed | tf_op | source)
XLA Modules:
  0.0 44.7 jit_solution(10537127872593496695)
XLA Ops:
  0.7 2.9 %whiten.1 = (bf16[4,16,640]{2,1,0:T(8,128)(2,1)}, bf16[4,16,640]{2,1,0:T(8,128)(2,1)}, bf16[4,16,640]{2,1,0:T(8,128)(2,1)}, bf16[4,16,640]{2,1,0:T(8,128)(2,1)},...) custom-call(s32[4,2,8]{2,1,0:T(2,128)} %bitcast.17, ...), custom_call_target="tpu_custom_call" | custom-call | tf_op jit(solution)/shard_map/whiten/pallas_call | solution.py:74
  3.5 0.0 copy-start
  3.5 1.3 %collective-permute-start.7 = (bf16[4,16,640]{2,1,0:T(8,128)(2,1)}, bf16[4,16,640]{2,1,0:T(8,128)(2,1)S(1)}, u32[]{:S(2)}, u32[]{:S(2)}) collective-permute-start(bf16[4,16,640]{2,1,0:T(8,128)(2,1)} %get-tuple-element.20), channel_id=1, source_target_pairs={{0,4},{4,0},{8,12},{12,8},{16,20},{20,16},{24,28},{28,24},{1,5},{5... | collective-permute-start | bytes 245768 | tf_op jit(solution)/shard_map/ppermute | solution.py:329
  4.8 1.3 %collective-permute-start.8 = (bf16[4,16,640]{2,1,0:T(8,128)(2,1)}, bf16[4,16,640]{2,1,0:T(8,128)(2,1)S(1)}, u32[]{:S(2)}, u32[]{:S(2)}) collective-permute-start(bf16[4,16,640]{2,1,0:T(8,128)(2,1)} %get-tuple-element.21), channel_id=1, source_target_pairs={{0,8},{4,12},{8,0},{12,4},{16,24},{20,28},{24,16},{28,20},{1,9},{5... | collective-permute-start | bytes 245768 | tf_op jit(solution)/shard_map/ppermute | solution.py:329
  6.1 0.1 collective-permute-start.9
  6.2 0.0 collective-permute-start
  6.2 3.3 %collective-permute-start.1 = (bf16[4,16,640]{2,1,0:T(8,128)(2,1)}, bf16[4,16,640]{2,1,0:T(8,128)(2,1)S(1)}, u32[]{:S(2)}, u32[]{:S(2)}) collective-permute-start(bf16[4,16,640]{2,1,0:T(8,128)(2,1)} %get-tuple-element.16), channel_id=1, source_target_pairs={{0,20},{4,16},{8,28},{12,24},{16,4},{20,0},{24,12},{28,8},{1,21},{... | collective-permute-start | bytes 245768 | tf_op jit(solution)/shard_map/ppermute | solution.py:329
  9.5 0.0 collective-permute-done.7
  9.5 0.2 collective-permute-start.2
  9.7 0.0 collective-permute-done.8
  9.7 1.3 %collective-permute-start.3 = (bf16[4,16,640]{2,1,0:T(8,128)(2,1)}, bf16[4,16,640]{2,1,0:T(8,128)(2,1)S(1)}, u32[]{:S(2)}, u32[]{:S(2)}) collective-permute-start(bf16[4,16,640]{2,1,0:T(8,128)(2,1)} %get-tuple-element.18), channel_id=1, source_target_pairs={{0,28},{4,24},{8,20},{12,16},{16,12},{20,8},{24,4},{28,0},{1,29},{... | collective-permute-start | bytes 245768 | tf_op jit(solution)/shard_map/ppermute | solution.py:329
  11.0 0.0 collective-permute-done.9
  11.0 0.9 %pad_maximum_fusion.1.refs_2_.refs_4_ = bf16[4,4,16,640]{3,2,1,0:T(8,128)(2,1)S(1)} fusion(bf16[1,4,16,640]{3,2,1,0:T(8,128)(2,1)S(1)} %bitcast.16, bf16[1,4,16,640]{3,2,1,0:T(8,128)(2,1)S(1)} %bitcast.14, bf16[1,4,16,640]{3,2,1,0:T(8,128)(2,1)S(1)} %bitcast.13, bf16[1,4,16,640]{3,2,1,0:T(8,128)(2,1)} %bitcast.10), kind=kLoop, calls=%fused_computation.1 | loop fusion | flops 491520 | bytes 655360 | tf_op jit(solution)/shard_map/stack | solution.py:334
  11.9 1.3 %collective-permute-start.11 = (bf16[4,4,16,640]{3,2,1,0:T(8,128)(2,1)S(1)}, bf16[4,4,16,640]{3,2,1,0:T(8,128)(2,1)S(1)}, u32[]{:S(2)}, u32[]{:S(2)}) collective-permute-start(bf16[4,4,16,640]{3,2,1,0:T(8,128)(2,1)S(1)} %pad_maximum_fusion.1.refs_2_.refs_4_), channel_id=1, source_target_pairs={{0,2},{1,3},{2,0},{3,1},{4,6},{5,7},{6,4},{7,5},{8,10},{9,11},{10,... | collective-permute-start | bytes 983048 | tf_op jit(solution)/shard_map/ppermute | solution.py:329
  13.2 0.0 collective-permute-done
  13.2 0.0 collective-permute-done.1
  13.2 8.1 %collective-permute-done.2 = bf16[4,16,640]{2,1,0:T(8,128)(2,1)S(1)} collective-permute-done((bf16[4,16,640]{2,1,0:T(8,128)(2,1)}, bf16[4,16,640]{2,1,0:T(8,128)(2,1)S(1)}, u32[]{:S(2)}, u32[]{:S(2)}) %collective-permute-start.2) | collective-permute-done | bytes 81952 | tf_op jit(solution)/shard_map/ppermute | solution.py:329
  21.3 3.4 %collective-permute-done.3 = bf16[4,16,640]{2,1,0:T(8,128)(2,1)S(1)} collective-permute-done((bf16[4,16,640]{2,1,0:T(8,128)(2,1)}, bf16[4,16,640]{2,1,0:T(8,128)(2,1)S(1)}, u32[]{:S(2)}, u32[]{:S(2)}) %collective-permute-start.3) | collective-permute-done | bytes 81952 | tf_op jit(solution)/shard_map/ppermute | solution.py:329
  24.8 0.1 pad_maximum_fusion.refs_0_
  24.8 1.3 %collective-permute-start.5 = (bf16[4,4,16,640]{3,2,1,0:T(8,128)(2,1)S(1)}, bf16[4,4,16,640]{3,2,1,0:T(8,128)(2,1)S(1)}, u32[]{:S(2)}, u32[]{:S(2)}) collective-permute-start(bf16[4,4,16,640]{3,2,1,0:T(8,128)(2,1)S(1)} %pad_maximum_fusion.refs_0_), channel_id=1, source_target_pairs={{0,2},{1,3},{2,0},{3,1},{4,6},{5,7},{6,4},{7,5},{8,10},{9,11},{10,... | collective-permute-start | bytes 983048 | tf_op jit(solution)/shard_map/ppermute | solution.py:329
  26.1 1.0 %collective-permute-start.10 = (bf16[4,4,16,640]{3,2,1,0:T(8,128)(2,1)S(1)}, bf16[4,4,16,640]{3,2,1,0:T(8,128)(2,1)S(1)}, u32[]{:S(2)}, u32[]{:S(2)}) collective-permute-start(bf16[4,4,16,640]{3,2,1,0:T(8,128)(2,1)S(1)} %pad_maximum_fusion.1.refs_2_.refs_4_), channel_id=1, source_target_pairs={{0,1},{1,0},{2,3},{3,2},{4,5},{5,4},{6,7},{7,6},{8,9},{9,8},{10,11... | collective-permute-start | bytes 983048 | tf_op jit(solution)/shard_map/ppermute | solution.py:329
  27.2 0.0 collective-permute-start.4
  27.2 0.0 collective-permute-done.11.refs_6_
  27.2 0.5 %collective-permute-start.12 = (bf16[4,4,16,640]{3,2,1,0:T(8,128)(2,1)S(1)}, bf16[4,4,16,640]{3,2,1,0:T(8,128)(2,1)S(1)}, u32[]{:S(2)}, u32[]{:S(2)}) collective-permute-start(bf16[4,4,16,640]{3,2,1,0:T(8,128)(2,1)S(1)} %collective-permute-done.11.refs_6_), channel_id=1, source_target_pairs={{0,1},{1,0},{2,3},{3,2},{4,5},{5,4},{6,7},{7,6},{8,9},{9,8},{10,11... | collective-permute-start | bytes 983048 | tf_op jit(solution)/shard_map/ppermute | solution.py:329
  27.7 5.8 %collective-permute-done.5.refs_2_ = bf16[4,4,16,640]{3,2,1,0:T(8,128)(2,1)S(1)} collective-permute-done((bf16[4,4,16,640]{3,2,1,0:T(8,128)(2,1)S(1)}, bf16[4,4,16,640]{3,2,1,0:T(8,128)(2,1)S(1)}, u32[]{:S(2)}, u32[]{:S(2)}) %collective-permute-start.5) | collective-permute-done | bytes 327712 | tf_op jit(solution)/shard_map/ppermute | solution.py:329
  33.4 1.6 %collective-permute-start.6 = (bf16[4,4,16,640]{3,2,1,0:T(8,128)(2,1)S(1)}, bf16[4,4,16,640]{3,2,1,0:T(8,128)(2,1)S(1)}, u32[]{:S(2)}, u32[]{:S(2)}) collective-permute-start(bf16[4,4,16,640]{3,2,1,0:T(8,128)(2,1)S(1)} %collective-permute-done.5.refs_2_), channel_id=1, source_target_pairs={{0,1},{1,0},{2,3},{3,2},{4,5},{5,4},{6,7},{7,6},{8,9},{9,8},{10,11... | collective-permute-start | bytes 983048 | tf_op jit(solution)/shard_map/ppermute | solution.py:329
  35.0 0.0 collective-permute-done.10.refs_3_.refs_5_
  35.0 0.0 collective-permute-done.4.refs_1_
  35.0 2.5 %held.1.refs_8_ = f32[4,8,512,128]{3,2,1,0:T(8,128)S(1)} custom-call(bf16[4,4,16,640]{3,2,1,0:T(8,128)(2,1)S(1)} %pad_maximum_fusion.refs_0_, bf16[4,4,16,640]{3,2,1,0:T(8,128)(2,1)S(1)} %collective-permute-done.4.refs_1_, bf16[4,4,16,640]{3,2,1,0:T(8,128)(2,1)S(1)} %pad_maximum_fusion.1.refs_2_.refs_4_, ...), custom_call_target="tpu_custom_call" | custom-call | flops 2147483648 | bytes 8388608 | tf_op jit(solution)/shard_map/held/pallas_call | solution.py:280
  37.5 0.0 collective-permute-done.12.refs_7_
  37.5 0.0 collective-permute-done.6.refs_3_
  37.5 7.2 %stack.41 = f32[32,4,128,128]{3,2,1,0:T(8,128)} custom-call(f32[4,8,128]{2,1,0:T(8,128)S(1)} %copy-done, bf16[4,4,16,640]{3,2,1,0:T(8,128)(2,1)S(1)} %pad_maximum_fusion.refs_0_, bf16[4,4,16,640]{3,2,1,0:T(8,128)(2,1)S(1)} %collective-permute-done.4.refs_1_, bf16[4,4,16,640]{3,2,1,0:T(8,128)(2,1)S(1)} %collective-permute-done.5.refs_2_, ...), custom_call_target="tpu_custom_call" | custom-call | tf_op jit(solution)/shard_map/stack/pallas_call | solution.py:294
  (1 shorter events, 0.0 us)
Async XLA Ops:
  3.5 34.0 %copy-start = (f32[4,8,128]{2,1,0:T(8,128)S(1)}, f32[4,8,128]{2,1,0:T(8,128)}, u32[]{:S(2)}) copy-start(f32[4,8,128]{2,1,0:T(8,128)} %get-tuple-element.14.factor_hbm) | copy-start | bytes 49156
  3.5 6.0 %collective-permute-start.7 = (bf16[4,16,640]{2,1,0:T(8,128)(2,1)}, bf16[4,16,640]{2,1,0:T(8,128)(2,1)S(1)}, u32[]{:S(2)}, u32[]{:S(2)}) collective-permute-start(bf16[4,16,640]{2,1,0:T(8,128)(2,1)} %get-tuple-element.20), channel_id=1, source_target_pairs={{0,4},{4,0},{8,12},{12,8},{16,20},{20,16},{24,28},{28,24},{1,5},{5... | collective-permute-start | bytes 245768 | tf_op jit(solution)/shard_map/ppermute | solution.py:329
  4.8 4.9 %collective-permute-start.8 = (bf16[4,16,640]{2,1,0:T(8,128)(2,1)}, bf16[4,16,640]{2,1,0:T(8,128)(2,1)S(1)}, u32[]{:S(2)}, u32[]{:S(2)}) collective-permute-start(bf16[4,16,640]{2,1,0:T(8,128)(2,1)} %get-tuple-element.21), channel_id=1, source_target_pairs={{0,8},{4,12},{8,0},{12,4},{16,24},{20,28},{24,16},{28,20},{1,9},{5... | collective-permute-start | bytes 245768 | tf_op jit(solution)/shard_map/ppermute | solution.py:329
  6.1 4.9 %collective-permute-start.9 = (bf16[4,16,640]{2,1,0:T(8,128)(2,1)}, bf16[4,16,640]{2,1,0:T(8,128)(2,1)S(1)}, u32[]{:S(2)}, u32[]{:S(2)}) collective-permute-start(bf16[4,16,640]{2,1,0:T(8,128)(2,1)} %get-tuple-element.22), channel_id=1, source_target_pairs={{0,12},{4,8},{8,4},{12,0},{16,28},{20,24},{24,20},{28,16},{1,13},{... | collective-permute-start | bytes 245768 | tf_op jit(solution)/shard_map/ppermute | solution.py:329
  6.2 7.0 %collective-permute-start = (bf16[4,16,640]{2,1,0:T(8,128)(2,1)}, bf16[4,16,640]{2,1,0:T(8,128)(2,1)S(1)}, u32[]{:S(2)}, u32[]{:S(2)}) collective-permute-start(bf16[4,16,640]{2,1,0:T(8,128)(2,1)} %get-tuple-element.15), channel_id=1, source_target_pairs={{0,16},{4,20},{8,24},{12,28},{16,0},{20,4},{24,8},{28,12},{1,17},{... | collective-permute-start | bytes 245768 | tf_op jit(solution)/shard_map/ppermute | solution.py:329
  6.2 7.0 %collective-permute-start.1 = (bf16[4,16,640]{2,1,0:T(8,128)(2,1)}, bf16[4,16,640]{2,1,0:T(8,128)(2,1)S(1)}, u32[]{:S(2)}, u32[]{:S(2)}) collective-permute-start(bf16[4,16,640]{2,1,0:T(8,128)(2,1)} %get-tuple-element.16), channel_id=1, source_target_pairs={{0,20},{4,16},{8,28},{12,24},{16,4},{20,0},{24,12},{28,8},{1,21},{... | collective-permute-start | bytes 245768 | tf_op jit(solution)/shard_map/ppermute | solution.py:329
  9.5 11.8 %collective-permute-start.2 = (bf16[4,16,640]{2,1,0:T(8,128)(2,1)}, bf16[4,16,640]{2,1,0:T(8,128)(2,1)S(1)}, u32[]{:S(2)}, u32[]{:S(2)}) collective-permute-start(bf16[4,16,640]{2,1,0:T(8,128)(2,1)} %get-tuple-element.17), channel_id=1, source_target_pairs={{0,24},{4,28},{8,16},{12,20},{16,8},{20,12},{24,0},{28,4},{1,25},{... | collective-permute-start | bytes 245768 | tf_op jit(solution)/shard_map/ppermute | solution.py:329
  9.7 15.1 %collective-permute-start.3 = (bf16[4,16,640]{2,1,0:T(8,128)(2,1)}, bf16[4,16,640]{2,1,0:T(8,128)(2,1)S(1)}, u32[]{:S(2)}, u32[]{:S(2)}) collective-permute-start(bf16[4,16,640]{2,1,0:T(8,128)(2,1)} %get-tuple-element.18), channel_id=1, source_target_pairs={{0,28},{4,24},{8,20},{12,16},{16,12},{20,8},{24,4},{28,0},{1,29},{... | collective-permute-start | bytes 245768 | tf_op jit(solution)/shard_map/ppermute | solution.py:329
  11.9 15.2 %collective-permute-start.11 = (bf16[4,4,16,640]{3,2,1,0:T(8,128)(2,1)S(1)}, bf16[4,4,16,640]{3,2,1,0:T(8,128)(2,1)S(1)}, u32[]{:S(2)}, u32[]{:S(2)}) collective-permute-start(bf16[4,4,16,640]{3,2,1,0:T(8,128)(2,1)S(1)} %pad_maximum_fusion.1.refs_2_.refs_4_), channel_id=1, source_target_pairs={{0,2},{1,3},{2,0},{3,1},{4,6},{5,7},{6,4},{7,5},{8,10},{9,11},{10,... | collective-permute-start | bytes 983048 | tf_op jit(solution)/shard_map/ppermute | solution.py:329
  24.8 8.6 %collective-permute-start.5 = (bf16[4,4,16,640]{3,2,1,0:T(8,128)(2,1)S(1)}, bf16[4,4,16,640]{3,2,1,0:T(8,128)(2,1)S(1)}, u32[]{:S(2)}, u32[]{:S(2)}) collective-permute-start(bf16[4,4,16,640]{3,2,1,0:T(8,128)(2,1)S(1)} %pad_maximum_fusion.refs_0_), channel_id=1, source_target_pairs={{0,2},{1,3},{2,0},{3,1},{4,6},{5,7},{6,4},{7,5},{8,10},{9,11},{10,... | collective-permute-start | bytes 983048 | tf_op jit(solution)/shard_map/ppermute | solution.py:329
  26.1 8.9 %collective-permute-start.10 = (bf16[4,4,16,640]{3,2,1,0:T(8,128)(2,1)S(1)}, bf16[4,4,16,640]{3,2,1,0:T(8,128)(2,1)S(1)}, u32[]{:S(2)}, u32[]{:S(2)}) collective-permute-start(bf16[4,4,16,640]{3,2,1,0:T(8,128)(2,1)S(1)} %pad_maximum_fusion.1.refs_2_.refs_4_), channel_id=1, source_target_pairs={{0,1},{1,0},{2,3},{3,2},{4,5},{5,4},{6,7},{7,6},{8,9},{9,8},{10,11... | collective-permute-start | bytes 983048 | tf_op jit(solution)/shard_map/ppermute | solution.py:329
  27.2 7.9 %collective-permute-start.4 = (bf16[4,4,16,640]{3,2,1,0:T(8,128)(2,1)S(1)}, bf16[4,4,16,640]{3,2,1,0:T(8,128)(2,1)S(1)}, u32[]{:S(2)}, u32[]{:S(2)}) collective-permute-start(bf16[4,4,16,640]{3,2,1,0:T(8,128)(2,1)S(1)} %pad_maximum_fusion.refs_0_), channel_id=1, source_target_pairs={{0,1},{1,0},{2,3},{3,2},{4,5},{5,4},{6,7},{7,6},{8,9},{9,8},{10,11... | collective-permute-start | bytes 983048 | tf_op jit(solution)/shard_map/ppermute | solution.py:329
  27.2 10.4 %collective-permute-start.12 = (bf16[4,4,16,640]{3,2,1,0:T(8,128)(2,1)S(1)}, bf16[4,4,16,640]{3,2,1,0:T(8,128)(2,1)S(1)}, u32[]{:S(2)}, u32[]{:S(2)}) collective-permute-start(bf16[4,4,16,640]{3,2,1,0:T(8,128)(2,1)S(1)} %collective-permute-done.11.refs_6_), channel_id=1, source_target_pairs={{0,1},{1,0},{2,3},{3,2},{4,5},{5,4},{6,7},{7,6},{8,9},{9,8},{10,11... | collective-permute-start | bytes 983048 | tf_op jit(solution)/shard_map/ppermute | solution.py:329
  33.4 4.1 %collective-permute-start.6 = (bf16[4,4,16,640]{3,2,1,0:T(8,128)(2,1)S(1)}, bf16[4,4,16,640]{3,2,1,0:T(8,128)(2,1)S(1)}, u32[]{:S(2)}, u32[]{:S(2)}) collective-permute-start(bf16[4,4,16,640]{3,2,1,0:T(8,128)(2,1)S(1)} %collective-permute-done.5.refs_2_), channel_id=1, source_target_pairs={{0,1},{1,0},{2,3},{3,2},{4,5},{5,4},{6,7},{7,6},{8,9},{9,8},{10,11... | collective-permute-start | bytes 983048 | tf_op jit(solution)/shard_map/ppermute | solution.py:329

commit v5 on v4

--- a/solution.py
+++ b/solution.py
@@ -13,6 +13,8 @@
 EPS = 1e-06
 STEP = 16
 WHITEN_VMEM = 60 << 20
+NEAR = (0, 1, 2, 4)
+FAR = (3, 5, 6, 7)
 
 
 def whiten_kernel(pairs_hbm, slot_hbm, offset_hbm, raw_hbm, *refs, scale):
@@ -92,11 +94,12 @@
 
 
 def unit(far, near, owner, t, j, lanes):
-    half, _, n, _ = near.shape
+    n = near.shape[2]
     k = owner ^ j
-    here = (k < half).astype(jnp.int32) * jnp.ones((n, 1), jnp.int32) > 0
-    at = k & (half - 1)
-    return jnp.where(here, near[at, t, :, lanes], far[at, t, :, lanes])
+    here = ((k & (k - 1)) == 0).astype(jnp.int32) * jnp.ones((n, 1), jnp.int32) > 0
+    in_near = jnp.minimum(k - (k >> 2), len(NEAR) - 1)
+    in_far = jnp.maximum(k - len(NEAR), 0)
+    return jnp.where(here, near[in_near, t, :, lanes], far[in_far, t, :, lanes])
 
 
 def second_block(far, near, owner, t, lanes):
@@ -330,8 +333,8 @@
 
     units = [u if k == 0 else swap(u, "pairs", owners, k) for k, u in enumerate(units)]
     held, brought = [], []
-    for low in (owners // 2, 0):
-        own = jnp.stack(units[low : low + owners // 2])
+    for group in (FAR, NEAR):
+        own = jnp.stack([units[k] for k in group])
         other = swap(own, "win", windows, 2)
         held.append((own, swap(own, "win", windows, 1)))
         brought.append((other, swap(other, "win", windows, 1)))

time: 44.9 us -> 42.7 us (0.951)
  waiting for transfers between devices: 17.3 us -> 14.5 us
  starting transfers between devices: 13.2 us -> 13.7 us
    ppermute x13, waiting for transfers between devices: 17.3 us -> 14.5 us  [swap(): return lax.ppermute(x, axis, [(i, i ^ k) for i in range(size)])]
    ppermute x13, starting transfers between devices: 13.2 us -> 13.7 us  [swap(): return lax.ppermute(x, axis, [(i, i ^ k) for i in range(size)])]
  transfers between devices with their start and end apart: 13 -> 13, of which waited for: 3 -> 4; matrix products, arithmetic and copies ran while one was open for 2% -> 2% of each run, Pallas kernels for 6% -> 6%
where the time goes in v5:
time: 42.7 us; the launch traced here: 42.5 us
  waiting for transfers between devices  14.5 us (34%)
  starting transfers between devices  13.7 us (32%)
  Pallas kernels  12.6 us (30%)
  other arithmetic  0.99 us (2%)
  between operations  0.72 us (2%)
    ppermute x13, waiting for transfers between devices, swap(): return lax.ppermute(x, axis, [(i, i ^ k) for i in range(size)])  14.5 us
    ppermute x13, starting transfers between devices, swap(): return lax.ppermute(x, axis, [(i, i ^ k) for i in range(size)])  13.7 us
    pallas_call x1, Pallas kernels, stack(): pl.pallas_call(functools.partial(stack_kernel, windows=windows), in_specs...  7.24 us
    pallas_call x1, Pallas kernels, whiten_and_pack(): pl.pallas_call(functools.partial(whiten_kernel, scale=scale), in_specs=[p...  2.85 us
    pallas_call x1, Pallas kernels, stack(): pl.pallas_call(functools.partial(held_kernel, windows=old), in_specs=[vme...  2.48 us
    another operation x2, other arithmetic, body(): own = jnp.stack([units[k] for k in group])  0.99 us
  transfers between devices with their start and end apart: 13, of which 4 were waited for; matrix products, arithmetic and copies ran while one was open for 2% of the time, Pallas kernels for 6%

profile of v5, /device:TPU:17, one launch (start us, length us, event | category | flops | bytes accessed | tf_op | source)
XLA Modules:
  0.0 42.5 jit_solution(10514575351052232512)
XLA Ops:
  0.7 2.9 %whiten.1 = (bf16[4,16,640]{2,1,0:T(8,128)(2,1)}, bf16[4,16,640]{2,1,0:T(8,128)(2,1)}, bf16[4,16,640]{2,1,0:T(8,128)(2,1)}, bf16[4,16,640]{2,1,0:T(8,128)(2,1)},...) custom-call(s32[4,2,8]{2,1,0:T(2,128)} %bitcast.17, ...), custom_call_target="tpu_custom_call" | custom-call | tf_op jit(solution)/shard_map/whiten/pallas_call | solution.py:76
  3.5 0.0 copy-start
  3.5 1.3 %collective-permute-start.7 = (bf16[4,16,640]{2,1,0:T(8,128)(2,1)}, bf16[4,16,640]{2,1,0:T(8,128)(2,1)S(1)}, u32[]{:S(2)}, u32[]{:S(2)}) collective-permute-start(bf16[4,16,640]{2,1,0:T(8,128)(2,1)} %get-tuple-element.20), channel_id=1, source_target_pairs={{0,4},{4,0},{8,12},{12,8},{16,20},{20,16},{24,28},{28,24},{1,5},{5... | collective-permute-start | bytes 245768 | tf_op jit(solution)/shard_map/ppermute | solution.py:332
  4.8 1.3 %collective-permute-start.8 = (bf16[4,16,640]{2,1,0:T(8,128)(2,1)}, bf16[4,16,640]{2,1,0:T(8,128)(2,1)S(1)}, u32[]{:S(2)}, u32[]{:S(2)}) collective-permute-start(bf16[4,16,640]{2,1,0:T(8,128)(2,1)} %get-tuple-element.21), channel_id=1, source_target_pairs={{0,8},{4,12},{8,0},{12,4},{16,24},{20,28},{24,16},{28,20},{1,9},{5... | collective-permute-start | bytes 245768 | tf_op jit(solution)/shard_map/ppermute | solution.py:332
  6.1 0.1 collective-permute-start.9
  6.2 0.1 collective-permute-start
  6.2 3.3 %collective-permute-start.1 = (bf16[4,16,640]{2,1,0:T(8,128)(2,1)}, bf16[4,16,640]{2,1,0:T(8,128)(2,1)S(1)}, u32[]{:S(2)}, u32[]{:S(2)}) collective-permute-start(bf16[4,16,640]{2,1,0:T(8,128)(2,1)} %get-tuple-element.16), channel_id=1, source_target_pairs={{0,20},{4,16},{8,28},{12,24},{16,4},{20,0},{24,12},{28,8},{1,21},{... | collective-permute-start | bytes 245768 | tf_op jit(solution)/shard_map/ppermute | solution.py:332
  9.5 0.0 collective-permute-done.7
  9.5 0.2 collective-permute-start.2
  9.7 0.0 collective-permute-done.8
  9.7 1.3 %collective-permute-start.3 = (bf16[4,16,640]{2,1,0:T(8,128)(2,1)}, bf16[4,16,640]{2,1,0:T(8,128)(2,1)S(1)}, u32[]{:S(2)}, u32[]{:S(2)}) collective-permute-start(bf16[4,16,640]{2,1,0:T(8,128)(2,1)} %get-tuple-element.18), channel_id=1, source_target_pairs={{0,28},{4,24},{8,20},{12,16},{16,12},{20,8},{24,4},{28,0},{1,29},{... | collective-permute-start | bytes 245768 | tf_op jit(solution)/shard_map/ppermute | solution.py:332
  11.0 0.0 collective-permute-done.9
  11.0 0.9 %pad_maximum_fusion.1.refs_2_.refs_4_ = bf16[4,4,16,640]{3,2,1,0:T(8,128)(2,1)S(1)} fusion(bf16[1,4,16,640]{3,2,1,0:T(8,128)(2,1)S(1)} %bitcast.16, bf16[1,4,16,640]{3,2,1,0:T(8,128)(2,1)S(1)} %bitcast.14, bf16[1,4,16,640]{3,2,1,0:T(8,128)(2,1)S(1)} %bitcast.13, bf16[1,4,16,640]{3,2,1,0:T(8,128)(2,1)} %bitcast.10), kind=kLoop, calls=%fused_computation.1 | loop fusion | flops 491520 | bytes 655360 | tf_op jit(solution)/shard_map/stack | solution.py:337
  11.9 1.3 %collective-permute-start.11 = (bf16[4,4,16,640]{3,2,1,0:T(8,128)(2,1)S(1)}, bf16[4,4,16,640]{3,2,1,0:T(8,128)(2,1)S(1)}, u32[]{:S(2)}, u32[]{:S(2)}) collective-permute-start(bf16[4,4,16,640]{3,2,1,0:T(8,128)(2,1)S(1)} %pad_maximum_fusion.1.refs_2_.refs_4_), channel_id=1, source_target_pairs={{0,2},{1,3},{2,0},{3,1},{4,6},{5,7},{6,4},{7,5},{8,10},{9,11},{10,... | collective-permute-start | bytes 983048 | tf_op jit(solution)/shard_map/ppermute | solution.py:332
  13.2 0.0 collective-permute-done
  13.2 0.4 %collective-permute-done.1 = bf16[4,16,640]{2,1,0:T(8,128)(2,1)S(1)} collective-permute-done((bf16[4,16,640]{2,1,0:T(8,128)(2,1)}, bf16[4,16,640]{2,1,0:T(8,128)(2,1)S(1)}, u32[]{:S(2)}, u32[]{:S(2)}) %collective-permute-start.1) | collective-permute-done | bytes 81952 | tf_op jit(solution)/shard_map/ppermute | solution.py:332
  13.7 7.1 %collective-permute-done.2 = bf16[4,16,640]{2,1,0:T(8,128)(2,1)S(1)} collective-permute-done((bf16[4,16,640]{2,1,0:T(8,128)(2,1)}, bf16[4,16,640]{2,1,0:T(8,128)(2,1)S(1)}, u32[]{:S(2)}, u32[]{:S(2)}) %collective-permute-start.2) | collective-permute-done | bytes 81952 | tf_op jit(solution)/shard_map/ppermute | solution.py:332
  20.7 1.7 %collective-permute-done.3 = bf16[4,16,640]{2,1,0:T(8,128)(2,1)S(1)} collective-permute-done((bf16[4,16,640]{2,1,0:T(8,128)(2,1)}, bf16[4,16,640]{2,1,0:T(8,128)(2,1)S(1)}, u32[]{:S(2)}, u32[]{:S(2)}) %collective-permute-start.3) | collective-permute-done | bytes 81952 | tf_op jit(solution)/shard_map/ppermute | solution.py:332
  22.5 0.1 pad_maximum_fusion.refs_0_
  22.5 1.3 %collective-permute-start.5 = (bf16[4,4,16,640]{3,2,1,0:T(8,128)(2,1)S(1)}, bf16[4,4,16,640]{3,2,1,0:T(8,128)(2,1)S(1)}, u32[]{:S(2)}, u32[]{:S(2)}) collective-permute-start(bf16[4,4,16,640]{3,2,1,0:T(8,128)(2,1)S(1)} %pad_maximum_fusion.refs_0_), channel_id=1, source_target_pairs={{0,2},{1,3},{2,0},{3,1},{4,6},{5,7},{6,4},{7,5},{8,10},{9,11},{10,... | collective-permute-start | bytes 983048 | tf_op jit(solution)/shard_map/ppermute | solution.py:332
  23.8 1.3 %collective-permute-start.10 = (bf16[4,4,16,640]{3,2,1,0:T(8,128)(2,1)S(1)}, bf16[4,4,16,640]{3,2,1,0:T(8,128)(2,1)S(1)}, u32[]{:S(2)}, u32[]{:S(2)}) collective-permute-start(bf16[4,4,16,640]{3,2,1,0:T(8,128)(2,1)S(1)} %pad_maximum_fusion.1.refs_2_.refs_4_), channel_id=1, source_target_pairs={{0,1},{1,0},{2,3},{3,2},{4,5},{5,4},{6,7},{7,6},{8,9},{9,8},{10,11... | collective-permute-start | bytes 983048 | tf_op jit(solution)/shard_map/ppermute | solution.py:332
  25.1 0.0 collective-permute-start.4
  25.1 0.0 collective-permute-done.11.refs_6_
  25.1 0.5 %collective-permute-start.12 = (bf16[4,4,16,640]{3,2,1,0:T(8,128)(2,1)S(1)}, bf16[4,4,16,640]{3,2,1,0:T(8,128)(2,1)S(1)}, u32[]{:S(2)}, u32[]{:S(2)}) collective-permute-start(bf16[4,4,16,640]{3,2,1,0:T(8,128)(2,1)S(1)} %collective-permute-done.11.refs_6_), channel_id=1, source_target_pairs={{0,1},{1,0},{2,3},{3,2},{4,5},{5,4},{6,7},{7,6},{8,9},{9,8},{10,11... | collective-permute-start | bytes 983048 | tf_op jit(solution)/shard_map/ppermute | solution.py:332
  25.6 5.2 %collective-permute-done.5.refs_2_ = bf16[4,4,16,640]{3,2,1,0:T(8,128)(2,1)S(1)} collective-permute-done((bf16[4,4,16,640]{3,2,1,0:T(8,128)(2,1)S(1)}, bf16[4,4,16,640]{3,2,1,0:T(8,128)(2,1)S(1)}, u32[]{:S(2)}, u32[]{:S(2)}) %collective-permute-start.5) | collective-permute-done | bytes 327712 | tf_op jit(solution)/shard_map/ppermute | solution.py:332
  30.8 1.9 %collective-permute-start.6 = (bf16[4,4,16,640]{3,2,1,0:T(8,128)(2,1)S(1)}, bf16[4,4,16,640]{3,2,1,0:T(8,128)(2,1)S(1)}, u32[]{:S(2)}, u32[]{:S(2)}) collective-permute-start(bf16[4,4,16,640]{3,2,1,0:T(8,128)(2,1)S(1)} %collective-permute-done.5.refs_2_), channel_id=1, source_target_pairs={{0,1},{1,0},{2,3},{3,2},{4,5},{5,4},{6,7},{7,6},{8,9},{9,8},{10,11... | collective-permute-start | bytes 983048 | tf_op jit(solution)/shard_map/ppermute | solution.py:332
  32.7 0.0 collective-permute-done.10.refs_3_.refs_5_
  32.7 0.0 collective-permute-done.4.refs_1_
  32.7 2.5 %held.1.refs_8_ = f32[4,8,512,128]{3,2,1,0:T(8,128)S(1)} custom-call(bf16[4,4,16,640]{3,2,1,0:T(8,128)(2,1)S(1)} %pad_maximum_fusion.refs_0_, bf16[4,4,16,640]{3,2,1,0:T(8,128)(2,1)S(1)} %collective-permute-done.4.refs_1_, bf16[4,4,16,640]{3,2,1,0:T(8,128)(2,1)S(1)} %pad_maximum_fusion.1.refs_2_.refs_4_, ...), custom_call_target="tpu_custom_call" | custom-call | flops 2147483648 | bytes 8388608 | tf_op jit(solution)/shard_map/held/pallas_call | solution.py:283
  35.2 0.0 collective-permute-done.12.refs_7_
  35.2 0.0 collective-permute-done.6.refs_3_
  35.2 7.2 %stack.41 = f32[32,4,128,128]{3,2,1,0:T(8,128)} custom-call(f32[4,8,128]{2,1,0:T(8,128)S(1)} %copy-done, bf16[4,4,16,640]{3,2,1,0:T(8,128)(2,1)S(1)} %pad_maximum_fusion.refs_0_, bf16[4,4,16,640]{3,2,1,0:T(8,128)(2,1)S(1)} %collective-permute-done.4.refs_1_, bf16[4,4,16,640]{3,2,1,0:T(8,128)(2,1)S(1)} %collective-permute-done.5.refs_2_, ...), custom_call_target="tpu_custom_call" | custom-call | tf_op jit(solution)/shard_map/stack/pallas_call | solution.py:297
  (1 shorter events, 0.0 us)
Async XLA Ops:
  3.5 31.7 %copy-start = (f32[4,8,128]{2,1,0:T(8,128)S(1)}, f32[4,8,128]{2,1,0:T(8,128)}, u32[]{:S(2)}) copy-start(f32[4,8,128]{2,1,0:T(8,128)} %get-tuple-element.14.factor_hbm) | copy-start | bytes 49156
  3.5 6.0 %collective-permute-start.7 = (bf16[4,16,640]{2,1,0:T(8,128)(2,1)}, bf16[4,16,640]{2,1,0:T(8,128)(2,1)S(1)}, u32[]{:S(2)}, u32[]{:S(2)}) collective-permute-start(bf16[4,16,640]{2,1,0:T(8,128)(2,1)} %get-tuple-element.20), channel_id=1, source_target_pairs={{0,4},{4,0},{8,12},{12,8},{16,20},{20,16},{24,28},{28,24},{1,5},{5... | collective-permute-start | bytes 245768 | tf_op jit(solution)/shard_map/ppermute | solution.py:332
  4.8 4.9 %collective-permute-start.8 = (bf16[4,16,640]{2,1,0:T(8,128)(2,1)}, bf16[4,16,640]{2,1,0:T(8,128)(2,1)S(1)}, u32[]{:S(2)}, u32[]{:S(2)}) collective-permute-start(bf16[4,16,640]{2,1,0:T(8,128)(2,1)} %get-tuple-element.21), channel_id=1, source_target_pairs={{0,8},{4,12},{8,0},{12,4},{16,24},{20,28},{24,16},{28,20},{1,9},{5... | collective-permute-start | bytes 245768 | tf_op jit(solution)/shard_map/ppermute | solution.py:332
  6.1 4.9 %collective-permute-start.9 = (bf16[4,16,640]{2,1,0:T(8,128)(2,1)}, bf16[4,16,640]{2,1,0:T(8,128)(2,1)S(1)}, u32[]{:S(2)}, u32[]{:S(2)}) collective-permute-start(bf16[4,16,640]{2,1,0:T(8,128)(2,1)} %get-tuple-element.22), channel_id=1, source_target_pairs={{0,16},{4,20},{8,24},{12,28},{16,0},{20,4},{24,8},{28,12},{1,17},{... | collective-permute-start | bytes 245768 | tf_op jit(solution)/shard_map/ppermute | solution.py:332
  6.2 7.1 %collective-permute-start = (bf16[4,16,640]{2,1,0:T(8,128)(2,1)}, bf16[4,16,640]{2,1,0:T(8,128)(2,1)S(1)}, u32[]{:S(2)}, u32[]{:S(2)}) collective-permute-start(bf16[4,16,640]{2,1,0:T(8,128)(2,1)} %get-tuple-element.15), channel_id=1, source_target_pairs={{0,12},{4,8},{8,4},{12,0},{16,28},{20,24},{24,20},{28,16},{1,13},{... | collective-permute-start | bytes 245768 | tf_op jit(solution)/shard_map/ppermute | solution.py:332
  6.2 7.4 %collective-permute-start.1 = (bf16[4,16,640]{2,1,0:T(8,128)(2,1)}, bf16[4,16,640]{2,1,0:T(8,128)(2,1)S(1)}, u32[]{:S(2)}, u32[]{:S(2)}) collective-permute-start(bf16[4,16,640]{2,1,0:T(8,128)(2,1)} %get-tuple-element.16), channel_id=1, source_target_pairs={{0,20},{4,16},{8,28},{12,24},{16,4},{20,0},{24,12},{28,8},{1,21},{... | collective-permute-start | bytes 245768 | tf_op jit(solution)/shard_map/ppermute | solution.py:332
  9.5 11.2 %collective-permute-start.2 = (bf16[4,16,640]{2,1,0:T(8,128)(2,1)}, bf16[4,16,640]{2,1,0:T(8,128)(2,1)S(1)}, u32[]{:S(2)}, u32[]{:S(2)}) collective-permute-start(bf16[4,16,640]{2,1,0:T(8,128)(2,1)} %get-tuple-element.17), channel_id=1, source_target_pairs={{0,24},{4,28},{8,16},{12,20},{16,8},{20,12},{24,0},{28,4},{1,25},{... | collective-permute-start | bytes 245768 | tf_op jit(solution)/shard_map/ppermute | solution.py:332
  9.7 12.8 %collective-permute-start.3 = (bf16[4,16,640]{2,1,0:T(8,128)(2,1)}, bf16[4,16,640]{2,1,0:T(8,128)(2,1)S(1)}, u32[]{:S(2)}, u32[]{:S(2)}) collective-permute-start(bf16[4,16,640]{2,1,0:T(8,128)(2,1)} %get-tuple-element.18), channel_id=1, source_target_pairs={{0,28},{4,24},{8,20},{12,16},{16,12},{20,8},{24,4},{28,0},{1,29},{... | collective-permute-start | bytes 245768 | tf_op jit(solution)/shard_map/ppermute | solution.py:332
  11.9 13.2 %collective-permute-start.11 = (bf16[4,4,16,640]{3,2,1,0:T(8,128)(2,1)S(1)}, bf16[4,4,16,640]{3,2,1,0:T(8,128)(2,1)S(1)}, u32[]{:S(2)}, u32[]{:S(2)}) collective-permute-start(bf16[4,4,16,640]{3,2,1,0:T(8,128)(2,1)S(1)} %pad_maximum_fusion.1.refs_2_.refs_4_), channel_id=1, source_target_pairs={{0,2},{1,3},{2,0},{3,1},{4,6},{5,7},{6,4},{7,5},{8,10},{9,11},{10,... | collective-permute-start | bytes 983048 | tf_op jit(solution)/shard_map/ppermute | solution.py:332
  22.5 8.3 %collective-permute-start.5 = (bf16[4,4,16,640]{3,2,1,0:T(8,128)(2,1)S(1)}, bf16[4,4,16,640]{3,2,1,0:T(8,128)(2,1)S(1)}, u32[]{:S(2)}, u32[]{:S(2)}) collective-permute-start(bf16[4,4,16,640]{3,2,1,0:T(8,128)(2,1)S(1)} %pad_maximum_fusion.refs_0_), channel_id=1, source_target_pairs={{0,2},{1,3},{2,0},{3,1},{4,6},{5,7},{6,4},{7,5},{8,10},{9,11},{10,... | collective-permute-start | bytes 983048 | tf_op jit(solution)/shard_map/ppermute | solution.py:332
  23.8 8.9 %collective-permute-start.10 = (bf16[4,4,16,640]{3,2,1,0:T(8,128)(2,1)S(1)}, bf16[4,4,16,640]{3,2,1,0:T(8,128)(2,1)S(1)}, u32[]{:S(2)}, u32[]{:S(2)}) collective-permute-start(bf16[4,4,16,640]{3,2,1,0:T(8,128)(2,1)S(1)} %pad_maximum_fusion.1.refs_2_.refs_4_), channel_id=1, source_target_pairs={{0,1},{1,0},{2,3},{3,2},{4,5},{5,4},{6,7},{7,6},{8,9},{9,8},{10,11... | collective-permute-start | bytes 983048 | tf_op jit(solution)/shard_map/ppermute | solution.py:332
  25.1 7.6 %collective-permute-start.4 = (bf16[4,4,16,640]{3,2,1,0:T(8,128)(2,1)S(1)}, bf16[4,4,16,640]{3,2,1,0:T(8,128)(2,1)S(1)}, u32[]{:S(2)}, u32[]{:S(2)}) collective-permute-start(bf16[4,4,16,640]{3,2,1,0:T(8,128)(2,1)S(1)} %pad_maximum_fusion.refs_0_), channel_id=1, source_target_pairs={{0,1},{1,0},{2,3},{3,2},{4,5},{5,4},{6,7},{7,6},{8,9},{9,8},{10,11... | collective-permute-start | bytes 983048 | tf_op jit(solution)/shard_map/ppermute | solution.py:332
  25.1 10.1 %collective-permute-start.12 = (bf16[4,4,16,640]{3,2,1,0:T(8,128)(2,1)S(1)}, bf16[4,4,16,640]{3,2,1,0:T(8,128)(2,1)S(1)}, u32[]{:S(2)}, u32[]{:S(2)}) collective-permute-start(bf16[4,4,16,640]{3,2,1,0:T(8,128)(2,1)S(1)} %collective-permute-done.11.refs_6_), channel_id=1, source_target_pairs={{0,1},{1,0},{2,3},{3,2},{4,5},{5,4},{6,7},{7,6},{8,9},{9,8},{10,11... | collective-permute-start | bytes 983048 | tf_op jit(solution)/shard_map/ppermute | solution.py:332
  30.8 4.4 %collective-permute-start.6 = (bf16[4,4,16,640]{3,2,1,0:T(8,128)(2,1)S(1)}, bf16[4,4,16,640]{3,2,1,0:T(8,128)(2,1)S(1)}, u32[]{:S(2)}, u32[]{:S(2)}) collective-permute-start(bf16[4,4,16,640]{3,2,1,0:T(8,128)(2,1)S(1)} %collective-permute-done.5.refs_2_), channel_id=1, source_target_pairs={{0,1},{1,0},{2,3},{3,2},{4,5},{5,4},{6,7},{7,6},{8,9},{9,8},{10,11... | collective-permute-start | bytes 983048 | tf_op jit(solution)/shard_map/ppermute | solution.py:332
